TPU v7x, 32 devices: a whole 2x2x4 slice. The times are simulated.
32 devices in a mesh: circ: 4 (over z), radax: 8 (over y, x, core).
Axes of the slice: x: 2, y: 2, z: 4, core: 2. Of those that a mesh axis runs over, the one named last changes fastest.
Arguments:
- right_side: float32 [2048, 2048], P('circ', 'radax'), may hold values from -150 to 150
- coef_rotor: float32 [2048, 2048], P('circ', 'radax'), may hold values from 1.5 to 15
- coef_stator: float32 [2048, 2048], P('circ', 'radax'), may hold values from 1.5 to 15
- mortar_rows: int32 [2048], P('circ'), may hold values from 0 to 2047, as said below
- mortar_weight: float32 [2048], P('circ'), may hold values from 0.1 to 0.9
Outputs:
- solution_field: float32 [2048, 2048], P('circ', 'radax')
- residual: float32 [2048, 2048], P('circ', 'radax')
Inputs may be any that keep to these rules, and one draw needn't show every extreme that they name: (mortar_rows[s] - s - 1280) taken modulo 2048 lies in -3 to 3, and both ends occur.
All inputs are finite; a program needn't handle non-finite values.
Results may differ from a plain program's by a relative error of at most 0.0002.
Values sent between devices are 32-bit elements; how exact they have to be, the bound alone decides.
No kernel may reach another device: no remote copies, remote signals or barrier semaphores. Data moves between devices by JAX's collectives and lax.ppermute only.
A program may use at most 64 MiB of HBM per device.

v0:
```python
import jax
import jax.numpy as jnp
from jax import lax
from jax.sharding import PartitionSpec as P

W = 256
REACH = 3
SLIDE = 1280


def with_halo(cells, sides, width):
    for axis, dim in sides:
        count = lax.axis_size(axis)
        head = lax.slice_in_dim(cells, 0, width, axis=dim)
        tail = lax.slice_in_dim(cells, cells.shape[dim] - width, cells.shape[dim], axis=dim)
        cells = jnp.concatenate(
            [
                lax.ppermute(tail, axis, [(i, (i + 1) % count) for i in range(count)]),
                cells,
                lax.ppermute(head, axis, [((i + 1) % count, i) for i in range(count)]),
            ],
            axis=dim,
        )
    return cells


def shifted(block, axis, distance):
    devices = range(lax.axis_size(axis))
    route = [((i - distance) % len(devices), i) for i in devices]
    return lax.ppermute(block, axis, route)


def local(right_side, coef_rotor, coef_stator, mortar_rows, mortar_weight):
    row_count = right_side.shape[0]
    col_count = right_side.shape[1]
    cycle_size = lax.axis_size("circ")
    total_rows = row_count * cycle_size

    def stencil(grid_field, coef):
        padded = with_halo(grid_field, (("circ", 0),), 1)
        blocks = grid_field.reshape(grid_field.shape[0], col_count // W, W)
        side_pad = jnp.pad(blocks, ((0, 0), (0, 0), (1, 1)))
        beside = (side_pad[:, :, :-2] + side_pad[:, :, 2:]).reshape(grid_field.shape)
        return coef * grid_field - 0.25 * (padded[:-2] + padded[2:] + beside)

    margin = REACH + 1
    whole_sectors = SLIDE // row_count
    remainder = SLIDE % row_count
    stator_global = lax.axis_index("circ") * row_count + jnp.arange(row_count, dtype=jnp.int32)
    offset_int = (
        jnp.mod(mortar_rows - stator_global - SLIDE + total_rows // 2, total_rows) - total_rows // 2
    )
    offset_float = offset_int.astype(jnp.float32)
    plan = [
        (whole_sectors + 1, row_count - remainder, row_count),
        (whole_sectors, 0, row_count - remainder),
    ]
    coef_parts = []
    weight_parts = []
    offset_parts = []
    for shift_by, low_row, high_row in plan:
        got_coef, got_weight, got_offset = shifted(
            (
                coef_stator[low_row:high_row],
                mortar_weight[low_row:high_row],
                offset_float[low_row:high_row],
            ),
            "circ",
            shift_by,
        )
        coef_parts.append(got_coef)
        weight_parts.append(got_weight)
        offset_parts.append(got_offset)
    stator_coef = jnp.concatenate(coef_parts, axis=0)
    weight = jnp.concatenate(weight_parts, axis=0)[:, None]
    moved_offset = jnp.concatenate(offset_parts, axis=0).astype(jnp.int32)
    local_idx = jnp.arange(row_count, dtype=jnp.int32) + moved_offset + margin
    after_idx = local_idx + 1

    def project(trace):
        window = with_halo(trace, (("circ", 0),), margin)
        return weight * window[local_idx] + (1.0 - weight) * window[after_idx]

    def give_back(response):
        collect = jnp.zeros((row_count + 2 * margin, col_count), jnp.float32)
        collect = collect.at[local_idx].add(weight * response)
        collect = collect.at[after_idx].add((1.0 - weight) * response)
        summed = collect[margin : margin + row_count]
        for shift_by, portion in ((1, collect[margin + row_count :]), (-1, collect[:margin])):
            arrived = shifted(portion, "circ", shift_by)
            if shift_by == 1:
                summed = summed + jnp.pad(arrived, ((0, row_count - margin), (0, 0)))
            else:
                summed = summed + jnp.pad(arrived, ((row_count - margin, 0), (0, 0)))
        return summed

    def operator(trace):
        return stencil(trace, coef_rotor) + give_back(stencil(project(trace), stator_coef))

    image = operator(right_side)
    cross_one, gram_pp = lax.psum(
        (jnp.sum(right_side * image), jnp.sum(image * image)), ("circ", "radax")
    )
    second = operator(image)
    gram_pq, gram_qq, cross_two = lax.psum(
        (jnp.sum(image * second), jnp.sum(second * second), jnp.sum(right_side * second)),
        ("circ", "radax"),
    )
    determinant = gram_pp * gram_qq - gram_pq * gram_pq
    coeff_one = (gram_qq * cross_one - gram_pq * cross_two) / determinant
    coeff_two = (gram_pp * cross_two - gram_pq * cross_one) / determinant
    solution_field = coeff_one * right_side + coeff_two * image
    residual = right_side - coeff_one * image - coeff_two * second
    return (solution_field, residual)


def solution(mesh):
    return jax.shard_map(
        local,
        mesh=mesh,
        in_specs=(P("circ", "radax"), P("circ", "radax"), P("circ", "radax"), P("circ"), P("circ")),
        out_specs=(P("circ", "radax"), P("circ", "radax")),
        check_vma=False,
    )
```

profile of v0, /device:TPU:0, one launch (start us, length us, event | category | flops | bytes accessed | tf_op | source)
XLA Modules:
  0.0 134.7 jit_solution(12033167347573811865)
XLA Ops:
  0.6 0.7 copy-done.3
  1.3 5.1 %collective-permute-start.2 = (f32[256]{0:T(256)S(1)}, f32[256]{0:T(256)S(1)}, u32[]{:S(2)}, u32[]{:S(2)}) collective-permute-start(f32[256]{0:T(256)S(1)} %get-tuple-element.37), channel_id=1, source_target_pairs={{8,0},{16,8},{24,16},{0,24},{9,1},{17,9},{25,17},{1,25},{10,2},{18... | collective-permute-start | bytes 3080 | tf_op jit(solution)/shard_map/ppermute | solution.py:30
  6.4 0.7 fusion.57
  7.2 1.0 collective-permute-start.8
  8.2 2.8 %collective-permute-start.9 = (f32[4,256]{1,0:T(4,128)S(1)}, f32[4,256]{1,0:T(4,128)S(1)}, u32[]{:S(2)}, u32[]{:S(2)}) collective-permute-start(f32[4,256]{1,0:T(4,128)S(1)} %get-tuple-element.32), channel_id=1, source_target_pairs={{8,0},{16,8},{24,16},{0,24},{9,1},{17,9},{25,17},{1,25},{10,2},{18... | collective-permute-start | bytes 12296 | tf_op jit(solution)/shard_map/ppermute | solution.py:20
  11.0 0.7 collective-permute-start.4
  11.7 1.1 fusion.55
  12.7 1.9 %collective-permute-done.4 = f32[256]{0:T(256)S(1)} collective-permute-done((f32[256]{0:T(256)S(1)}, f32[256]{0:T(256)S(1)}, u32[]{:S(2)}, u32[]{:S(2)}) %collective-permute-start.4) | collective-permute-done | bytes 1056 | tf_op jit(solution)/shard_map/ppermute | solution.py:30
  14.6 1.1 collective-permute-start.5
  15.8 3.3 %collective-permute-done.5 = f32[256]{0:T(256)S(1)} collective-permute-done((f32[256]{0:T(256)S(1)}, f32[256]{0:T(256)S(1)}, u32[]{:S(2)}, u32[]{:S(2)}) %collective-permute-start.5) | collective-permute-done | bytes 1056 | tf_op jit(solution)/shard_map/ppermute | solution.py:30
  19.1 2.4 %collective-permute-start.6 = (f32[256,256]{1,0:T(8,128)S(1)}, f32[256,256]{1,0:T(8,128)S(1)}, u32[]{:S(2)}, u32[]{:S(2)}) collective-permute-start(f32[256,256]{1,0:T(8,128)S(1)} %get-tuple-element.28), channel_id=1, source_target_pairs={{8,0},{16,8},{24,16},{0,24},{9,1},{17,9},{25,17},{1,25},{10,2},{18... | collective-permute-start | bytes 786440 | tf_op jit(solution)/shard_map/ppermute | solution.py:30
  21.5 0.1 collective-permute-start.7
  21.7 1.6 %gather_fusion = f32[512,256]{1,0:T(8,128)S(1)} fusion(f32[520,256]{1,0:T(8,128)S(1)} %pad_maximum_fusion, s32[1024]{0:T(1024)S(1)} %get-tuple-element.40), kind=kCustom, calls=%fused_computation | custom fusion | bytes 1050624 | tf_op jit(solution)/shard_map/gather | solution.py:82
  23.3 1.6 %gather_fusion.1 = f32[512,256]{1,0:T(8,128)S(1)} fusion(f32[520,256]{1,0:T(8,128)S(1)} %pad_maximum_fusion, s32[1024]{0:T(1024)S(1)} %get-tuple-element.39), kind=kCustom, calls=%fused_computation.1 | custom fusion | bytes 1050624 | tf_op jit(solution)/shard_map/gather | solution.py:82
  24.9 0.2 multiply_add_fusion.2
  25.1 0.8 collective-permute-start.10
  25.9 3.1 %collective-permute-start.11 = (f32[1,256]{1,0:T(1,128)S(1)}, f32[1,256]{1,0:T(1,128)S(1)}, u32[]{:S(2)}, u32[]{:S(2)}) collective-permute-start(f32[1,256]{1,0:T(1,128)S(1)} %get-tuple-element.30), channel_id=1, source_target_pairs={{8,0},{16,8},{24,16},{0,24},{9,1},{17,9},{25,17},{1,25},{10,2},{18... | collective-permute-start | bytes 3080 | tf_op jit(solution)/shard_map/ppermute | solution.py:20
  29.0 0.2 fusion.29
  29.2 6.3 %collective-permute-done.7 = f32[256,256]{1,0:T(8,128)S(1)} collective-permute-done((f32[256,256]{1,0:T(8,128)S(1)}, f32[256,256]{1,0:T(8,128)S(1)}, u32[]{:S(2)}, u32[]{:S(2)}) %collective-permute-start.7) | collective-permute-done | bytes 262176 | tf_op jit(solution)/shard_map/ppermute | solution.py:30
  35.6 0.4 fusion.10
  36.0 3.5 %scatter_custom_fusion = f32[520,256]{1,0:T(8,128)S(1)} fusion(s32[512]{0:T(512)S(1)} %bitcast.65, f32[512,256]{1,0:T(8,128)S(1)} %fusion.10, f32[]{:T(128)} %constant.17.clone.1, f32[512]{0:T(512)S(1)} %constant_dynamic-update-slice_fusion), kind=kCustom, calls=%fused_computation.76 | custom fusion | flops 262144 | bytes 1058820 | tf_op jit(solution)/shard_map/scatter-add | solution.py:86
  39.5 0.0 copy-start.1
  39.5 3.6 %scatter_custom_fusion.1 = f32[520,256]{1,0:T(8,128)S(1)} fusion(f32[520,256]{1,0:T(8,128)S(1)} %scatter_custom_fusion, s32[512]{0:T(512)S(1)} %bitcast.62, f32[512,256]{1,0:T(8,128)S(1)} %fusion.10, f32[512]{0:T(512)S(1)} %broadcast_subtract_fusion), kind=kCustom, calls=%fused_computation.74 | custom fusion | flops 262144 | bytes 1058816 | tf_op jit(solution)/shard_map/scatter-add | solution.py:87
  43.2 0.6 collective-permute-start.12
  43.8 3.3 %collective-permute-start.13 = (f32[4,256]{1,0:T(4,128)S(1)}, f32[4,256]{1,0:T(4,128)S(1)}, u32[]{:S(2)}, u32[]{:S(2)}) collective-permute-start(f32[4,256]{1,0:T(4,128)S(1)} %get-tuple-element.18), channel_id=1, source_target_pairs={{8,0},{16,8},{24,16},{0,24},{9,1},{17,9},{25,17},{1,25},{10,2},{18... | collective-permute-start | bytes 12296 | tf_op jit(solution)/shard_map/ppermute | solution.py:30
  47.1 3.8 %collective-permute-start.1 = (f32[1,256]{1,0:T(1,128)S(1)}, f32[1,256]{1,0:T(1,128)S(1)}, u32[]{:S(2)}, u32[]{:S(2)}) collective-permute-start(f32[1,256]{1,0:T(1,128)S(1)} %get-tuple-element.26), channel_id=1, source_target_pairs={{8,0},{16,8},{24,16},{0,24},{9,1},{17,9},{25,17},{1,25},{10,2},{18... | collective-permute-start | bytes 3080 | tf_op jit(solution)/shard_map/ppermute | solution.py:20
  50.9 1.5 %collective-permute-done = f32[1,256]{1,0:T(1,128)S(1)} collective-permute-done((f32[1,256]{1,0:T(1,128)S(1)}, f32[1,256]{1,0:T(1,128)S(1)}, u32[]{:S(2)}, u32[]{:S(2)}) %collective-permute-start) | collective-permute-done | bytes 1056 | tf_op jit(solution)/shard_map/ppermute | solution.py:18
  52.5 0.4 fusion.5
  52.9 0.1 collective-permute-start.16
  52.9 3.9 %collective-permute-start.17 = (f32[4,256]{1,0:T(4,128)S(1)}, f32[4,256]{1,0:T(4,128)S(1)}, u32[]{:S(2)}, u32[]{:S(2)}) collective-permute-start(f32[4,256]{1,0:T(4,128)S(1)} %get-tuple-element.24), channel_id=1, source_target_pairs={{8,0},{16,8},{24,16},{0,24},{9,1},{17,9},{25,17},{1,25},{10,2},{18... | collective-permute-start | bytes 12296 | tf_op jit(solution)/shard_map/ppermute | solution.py:20
  56.8 1.5 %collective-permute-done.16 = f32[4,256]{1,0:T(4,128)S(1)} collective-permute-done((f32[4,256]{1,0:T(4,128)S(1)}, f32[4,256]{1,0:T(4,128)S(1)}, u32[]{:S(2)}, u32[]{:S(2)}) %collective-permute-start.16) | collective-permute-done | bytes 4128 | tf_op jit(solution)/shard_map/ppermute | solution.py:18
  58.4 1.6 %gather_fusion.2 = f32[512,256]{1,0:T(8,128)S(1)} fusion(f32[520,256]{1,0:T(8,128)S(1)} %pad_maximum_fusion.1, s32[1024]{0:T(1024)S(1)} %get-tuple-element.40), kind=kCustom, calls=%fused_computation.2 | custom fusion | bytes 1050624 | tf_op jit(solution)/shard_map/gather | solution.py:82
  59.9 1.6 %gather_fusion.3 = f32[512,256]{1,0:T(8,128)S(1)} fusion(f32[520,256]{1,0:T(8,128)S(1)} %pad_maximum_fusion.1, s32[1024]{0:T(1024)S(1)} %get-tuple-element.39), kind=kCustom, calls=%fused_computation.3 | custom fusion | bytes 1050624 | tf_op jit(solution)/shard_map/gather | solution.py:82
  61.5 0.2 multiply_add_fusion.1
  61.7 1.2 collective-permute-start.18
  62.9 3.0 %collective-permute-start.19 = (f32[1,256]{1,0:T(1,128)S(1)}, f32[1,256]{1,0:T(1,128)S(1)}, u32[]{:S(2)}, u32[]{:S(2)}) collective-permute-start(f32[1,256]{1,0:T(1,128)S(1)} %get-tuple-element.22), channel_id=1, source_target_pairs={{8,0},{16,8},{24,16},{0,24},{9,1},{17,9},{25,17},{1,25},{10,2},{18... | collective-permute-start | bytes 3080 | tf_op jit(solution)/shard_map/ppermute | solution.py:20
  65.9 0.2 fusion.28
  66.1 1.1 collective-permute-done.18
  67.2 0.4 fusion.21
  67.6 3.5 %scatter_custom_fusion.2 = f32[520,256]{1,0:T(8,128)S(1)} fusion(s32[512]{0:T(512)S(1)} %bitcast.66, f32[512,256]{1,0:T(8,128)S(1)} %fusion.21, f32[]{:T(128)} %constant.17.clone.1, f32[512]{0:T(512)S(1)} %constant_dynamic-update-slice_fusion), kind=kCustom, calls=%fused_computation.71 | custom fusion | flops 262144 | bytes 1058820 | tf_op jit(solution)/shard_map/scatter-add | solution.py:86
  71.1 3.6 %scatter_custom_fusion.3 = f32[520,256]{1,0:T(8,128)S(1)} fusion(f32[520,256]{1,0:T(8,128)S(1)} %scatter_custom_fusion.2, s32[512]{0:T(512)S(1)} %bitcast.63, f32[512,256]{1,0:T(8,128)S(1)} %fusion.21, f32[512]{0:T(512)S(1)} %broadcast_subtract_fusion), kind=kCustom, calls=%fused_computation.69 | custom fusion | flops 262144 | bytes 1058816 | tf_op jit(solution)/shard_map/scatter-add | solution.py:87
  74.8 1.3 collective-permute-start.20
  76.1 2.8 %collective-permute-start.21 = (f32[4,256]{1,0:T(4,128)S(1)}, f32[4,256]{1,0:T(4,128)S(1)}, u32[]{:S(2)}, u32[]{:S(2)}) collective-permute-start(f32[4,256]{1,0:T(4,128)S(1)} %get-tuple-element.16), channel_id=1, source_target_pairs={{8,0},{16,8},{24,16},{0,24},{9,1},{17,9},{25,17},{1,25},{10,2},{18... | collective-permute-start | bytes 12296 | tf_op jit(solution)/shard_map/ppermute | solution.py:30
  79.0 3.8 %collective-permute-start.15 = (f32[1,256]{1,0:T(1,128)S(1)}, f32[1,256]{1,0:T(1,128)S(1)}, u32[]{:S(2)}, u32[]{:S(2)}) collective-permute-start(f32[1,256]{1,0:T(1,128)S(1)} %get-tuple-element.20), channel_id=1, source_target_pairs={{8,0},{16,8},{24,16},{0,24},{9,1},{17,9},{25,17},{1,25},{10,2},{18... | collective-permute-start | bytes 3080 | tf_op jit(solution)/shard_map/ppermute | solution.py:20
  82.8 1.5 %collective-permute-done.14 = f32[1,256]{1,0:T(1,128)S(1)} collective-permute-done((f32[1,256]{1,0:T(1,128)S(1)}, f32[1,256]{1,0:T(1,128)S(1)}, u32[]{:S(2)}, u32[]{:S(2)}) %collective-permute-start.14) | collective-permute-done | bytes 1056 | tf_op jit(solution)/shard_map/ppermute | solution.py:18
  84.4 1.2 multiply_reduce_fusion.4
  85.6 40.5 %all-reduce.8 = (f32[]{:T(128)}, f32[]{:T(128)}, f32[]{:T(128)}, f32[]{:T(128)}, f32[]{:T(128)}) all-reduce(f32[]{:T(128)} %get-tuple-element.6, f32[]{:T(128)} %get-tuple-element.3, f32[]{:T(128)} %get-tuple-element.5, f32[]{:T(128)} %get-tuple-element.4, f32[]{:T(128)} %get-tuple-element.2), channel_id=1, replica_groups=mesh['circ'=4,'radax'=8] {'circ','radax'}, use_global_device_ids=true, to_apply=%region_13.14 | all-reduce | flops 5 | bytes 40 | tf_op jit(solution)/shard_map/psum | solution.py:101
  133.6 1.1 multiply_subtract_fusion
  (46 shorter events, 0.3 us)
Async XLA Ops:
  0.6 0.7 copy-start.3
  1.3 20.2 %collective-permute-start.2 = (f32[256]{0:T(256)S(1)}, f32[256]{0:T(256)S(1)}, u32[]{:S(2)}, u32[]{:S(2)}) collective-permute-start(f32[256]{0:T(256)S(1)} %get-tuple-element.37), channel_id=1, source_target_pairs={{8,0},{16,8},{24,16},{0,24},{9,1},{17,9},{25,17},{1,25},{10,2},{18... | collective-permute-start | bytes 3080 | tf_op jit(solution)/shard_map/ppermute | solution.py:30
  6.4 15.2 %collective-permute-start.3 = (f32[256]{0:T(256)S(1)}, f32[256]{0:T(256)S(1)}, u32[]{:S(2)}, u32[]{:S(2)}) collective-permute-start(f32[256]{0:T(256)S(1)} %get-tuple-element.38), channel_id=1, source_target_pairs={{16,0},{24,8},{0,16},{8,24},{17,1},{25,9},{1,17},{9,25},{18,2},{26... | collective-permute-start | bytes 3080 | tf_op jit(solution)/shard_map/ppermute | solution.py:30
  7.2 3.8 %copy-start.4 = (f32[512]{0:T(512)S(1)}, f32[512]{0:T(512)}, u32[]{:S(2)}) copy-start(f32[512]{0:T(512)} %param.9) | copy-start | bytes 6148
  7.2 14.5 %collective-permute-start.8 = (f32[4,256]{1,0:T(4,128)S(1)}, f32[4,256]{1,0:T(4,128)S(1)}, u32[]{:S(2)}, u32[]{:S(2)}) collective-permute-start(f32[4,256]{1,0:T(4,128)S(1)} %get-tuple-element.31), channel_id=1, source_target_pairs={{0,8},{8,16},{16,24},{24,0},{1,9},{9,17},{17,25},{25,1},{2,10},{10... | collective-permute-start | bytes 12296 | tf_op jit(solution)/shard_map/ppermute | solution.py:18
  8.2 13.5 %collective-permute-start.9 = (f32[4,256]{1,0:T(4,128)S(1)}, f32[4,256]{1,0:T(4,128)S(1)}, u32[]{:S(2)}, u32[]{:S(2)}) collective-permute-start(f32[4,256]{1,0:T(4,128)S(1)} %get-tuple-element.32), channel_id=1, source_target_pairs={{8,0},{16,8},{24,16},{0,24},{9,1},{17,9},{25,17},{1,25},{10,2},{18... | collective-permute-start | bytes 12296 | tf_op jit(solution)/shard_map/ppermute | solution.py:20
  11.0 10.7 %copy-start = (f32[512,256]{1,0:T(8,128)S(1)}, f32[512,256]{1,0:T(8,128)}, u32[]{:S(2)}) copy-start(f32[512,256]{1,0:T(8,128)} %param.5) | copy-start | bytes 1572868
  11.0 3.6 %collective-permute-start.4 = (f32[256]{0:T(256)S(1)}, f32[256]{0:T(256)S(1)}, u32[]{:S(2)}, u32[]{:S(2)}) collective-permute-start(f32[256]{0:T(256)S(1)} %get-tuple-element.34), channel_id=1, source_target_pairs={{8,0},{16,8},{24,16},{0,24},{9,1},{17,9},{25,17},{1,25},{10,2},{18... | collective-permute-start | bytes 3080 | tf_op jit(solution)/shard_map/ppermute | solution.py:30
  14.6 4.5 %collective-permute-start.5 = (f32[256]{0:T(256)S(1)}, f32[256]{0:T(256)S(1)}, u32[]{:S(2)}, u32[]{:S(2)}) collective-permute-start(f32[256]{0:T(256)S(1)} %get-tuple-element.33), channel_id=1, source_target_pairs={{16,0},{24,8},{0,16},{8,24},{17,1},{25,9},{1,17},{9,25},{18,2},{26... | collective-permute-start | bytes 3080 | tf_op jit(solution)/shard_map/ppermute | solution.py:30
  19.1 10.1 %collective-permute-start.6 = (f32[256,256]{1,0:T(8,128)S(1)}, f32[256,256]{1,0:T(8,128)S(1)}, u32[]{:S(2)}, u32[]{:S(2)}) collective-permute-start(f32[256,256]{1,0:T(8,128)S(1)} %get-tuple-element.28), channel_id=1, source_target_pairs={{8,0},{16,8},{24,16},{0,24},{9,1},{17,9},{25,17},{1,25},{10,2},{18... | collective-permute-start | bytes 786440 | tf_op jit(solution)/shard_map/ppermute | solution.py:30
  21.5 14.0 %collective-permute-start.7 = (f32[256,256]{1,0:T(8,128)S(1)}, f32[256,256]{1,0:T(8,128)S(1)}, u32[]{:S(2)}, u32[]{:S(2)}) collective-permute-start(f32[256,256]{1,0:T(8,128)S(1)} %get-tuple-element.27), channel_id=1, source_target_pairs={{16,0},{24,8},{0,16},{8,24},{17,1},{25,9},{1,17},{9,25},{18,2},{26... | collective-permute-start | bytes 786440 | tf_op jit(solution)/shard_map/ppermute | solution.py:30
  25.1 10.5 %collective-permute-start.10 = (f32[1,256]{1,0:T(1,128)S(1)}, f32[1,256]{1,0:T(1,128)S(1)}, u32[]{:S(2)}, u32[]{:S(2)}) collective-permute-start(f32[1,256]{1,0:T(1,128)S(1)} %get-tuple-element.29), channel_id=1, source_target_pairs={{0,8},{8,16},{16,24},{24,0},{1,9},{9,17},{17,25},{25,1},{2,10},{10... | collective-permute-start | bytes 3080 | tf_op jit(solution)/shard_map/ppermute | solution.py:18
  25.9 9.7 %collective-permute-start.11 = (f32[1,256]{1,0:T(1,128)S(1)}, f32[1,256]{1,0:T(1,128)S(1)}, u32[]{:S(2)}, u32[]{:S(2)}) collective-permute-start(f32[1,256]{1,0:T(1,128)S(1)} %get-tuple-element.30), channel_id=1, source_target_pairs={{8,0},{16,8},{24,16},{0,24},{9,1},{17,9},{25,17},{1,25},{10,2},{18... | collective-permute-start | bytes 3080 | tf_op jit(solution)/shard_map/ppermute | solution.py:20
  39.5 12.9 %copy-start.1 = (f32[512,256]{1,0:T(8,128)S(1)}, f32[512,256]{1,0:T(8,128)}, u32[]{:S(2)}) copy-start(f32[512,256]{1,0:T(8,128)} %param.6) | copy-start | bytes 1572868
  43.2 9.3 %collective-permute-start.12 = (f32[4,256]{1,0:T(4,128)S(1)}, f32[4,256]{1,0:T(4,128)S(1)}, u32[]{:S(2)}, u32[]{:S(2)}) collective-permute-start(f32[4,256]{1,0:T(4,128)S(1)} %get-tuple-element.17), channel_id=1, source_target_pairs={{24,0},{0,8},{8,16},{16,24},{25,1},{1,9},{9,17},{17,25},{26,2},{2,... | collective-permute-start | bytes 12296 | tf_op jit(solution)/shard_map/ppermute | solution.py:30
  43.8 8.7 %collective-permute-start.13 = (f32[4,256]{1,0:T(4,128)S(1)}, f32[4,256]{1,0:T(4,128)S(1)}, u32[]{:S(2)}, u32[]{:S(2)}) collective-permute-start(f32[4,256]{1,0:T(4,128)S(1)} %get-tuple-element.18), channel_id=1, source_target_pairs={{8,0},{16,8},{24,16},{0,24},{9,1},{17,9},{25,17},{1,25},{10,2},{18... | collective-permute-start | bytes 12296 | tf_op jit(solution)/shard_map/ppermute | solution.py:30
  47.1 5.4 %collective-permute-start = (f32[1,256]{1,0:T(1,128)S(1)}, f32[1,256]{1,0:T(1,128)S(1)}, u32[]{:S(2)}, u32[]{:S(2)}) collective-permute-start(f32[1,256]{1,0:T(1,128)S(1)} %get-tuple-element.25), channel_id=1, source_target_pairs={{0,8},{8,16},{16,24},{24,0},{1,9},{9,17},{17,25},{25,1},{2,10},{10... | collective-permute-start | bytes 3080 | tf_op jit(solution)/shard_map/ppermute | solution.py:18
  47.1 5.4 %collective-permute-start.1 = (f32[1,256]{1,0:T(1,128)S(1)}, f32[1,256]{1,0:T(1,128)S(1)}, u32[]{:S(2)}, u32[]{:S(2)}) collective-permute-start(f32[1,256]{1,0:T(1,128)S(1)} %get-tuple-element.26), channel_id=1, source_target_pairs={{8,0},{16,8},{24,16},{0,24},{9,1},{17,9},{25,17},{1,25},{10,2},{18... | collective-permute-start | bytes 3080 | tf_op jit(solution)/shard_map/ppermute | solution.py:20
  52.9 5.5 %collective-permute-start.16 = (f32[4,256]{1,0:T(4,128)S(1)}, f32[4,256]{1,0:T(4,128)S(1)}, u32[]{:S(2)}, u32[]{:S(2)}) collective-permute-start(f32[4,256]{1,0:T(4,128)S(1)} %get-tuple-element.23), channel_id=1, source_target_pairs={{0,8},{8,16},{16,24},{24,0},{1,9},{9,17},{17,25},{25,1},{2,10},{10... | collective-permute-start | bytes 12296 | tf_op jit(solution)/shard_map/ppermute | solution.py:18
  52.9 5.4 %collective-permute-start.17 = (f32[4,256]{1,0:T(4,128)S(1)}, f32[4,256]{1,0:T(4,128)S(1)}, u32[]{:S(2)}, u32[]{:S(2)}) collective-permute-start(f32[4,256]{1,0:T(4,128)S(1)} %get-tuple-element.24), channel_id=1, source_target_pairs={{8,0},{16,8},{24,16},{0,24},{9,1},{17,9},{25,17},{1,25},{10,2},{18... | collective-permute-start | bytes 12296 | tf_op jit(solution)/shard_map/ppermute | solution.py:20
  61.7 5.5 %collective-permute-start.18 = (f32[1,256]{1,0:T(1,128)S(1)}, f32[1,256]{1,0:T(1,128)S(1)}, u32[]{:S(2)}, u32[]{:S(2)}) collective-permute-start(f32[1,256]{1,0:T(1,128)S(1)} %get-tuple-element.21), channel_id=1, source_target_pairs={{0,8},{8,16},{16,24},{24,0},{1,9},{9,17},{17,25},{25,1},{2,10},{10... | collective-permute-start | bytes 3080 | tf_op jit(solution)/shard_map/ppermute | solution.py:18
  62.9 4.3 %collective-permute-start.19 = (f32[1,256]{1,0:T(1,128)S(1)}, f32[1,256]{1,0:T(1,128)S(1)}, u32[]{:S(2)}, u32[]{:S(2)}) collective-permute-start(f32[1,256]{1,0:T(1,128)S(1)} %get-tuple-element.22), channel_id=1, source_target_pairs={{8,0},{16,8},{24,16},{0,24},{9,1},{17,9},{25,17},{1,25},{10,2},{18... | collective-permute-start | bytes 3080 | tf_op jit(solution)/shard_map/ppermute | solution.py:20
  71.1 13.2 %copy-start.2 = (f32[512,256]{1,0:T(8,128)S(1)}, f32[512,256]{1,0:T(8,128)}, u32[]{:S(2)}) copy-start(f32[512,256]{1,0:T(8,128)} %param.6) | copy-start | bytes 1572868
  74.8 9.6 %collective-permute-start.20 = (f32[4,256]{1,0:T(4,128)S(1)}, f32[4,256]{1,0:T(4,128)S(1)}, u32[]{:S(2)}, u32[]{:S(2)}) collective-permute-start(f32[4,256]{1,0:T(4,128)S(1)} %get-tuple-element.15), channel_id=1, source_target_pairs={{24,0},{0,8},{8,16},{16,24},{25,1},{1,9},{9,17},{17,25},{26,2},{2,... | collective-permute-start | bytes 12296 | tf_op jit(solution)/shard_map/ppermute | solution.py:30
  76.1 8.2 %collective-permute-start.21 = (f32[4,256]{1,0:T(4,128)S(1)}, f32[4,256]{1,0:T(4,128)S(1)}, u32[]{:S(2)}, u32[]{:S(2)}) collective-permute-start(f32[4,256]{1,0:T(4,128)S(1)} %get-tuple-element.16), channel_id=1, source_target_pairs={{8,0},{16,8},{24,16},{0,24},{9,1},{17,9},{25,17},{1,25},{10,2},{18... | collective-permute-start | bytes 12296 | tf_op jit(solution)/shard_map/ppermute | solution.py:30
  79.0 5.4 %collective-permute-start.14 = (f32[1,256]{1,0:T(1,128)S(1)}, f32[1,256]{1,0:T(1,128)S(1)}, u32[]{:S(2)}, u32[]{:S(2)}) collective-permute-start(f32[1,256]{1,0:T(1,128)S(1)} %get-tuple-element.19), channel_id=1, source_target_pairs={{0,8},{8,16},{16,24},{24,0},{1,9},{9,17},{17,25},{25,1},{2,10},{10... | collective-permute-start | bytes 3080 | tf_op jit(solution)/shard_map/ppermute | solution.py:18
  79.0 5.4 %collective-permute-start.15 = (f32[1,256]{1,0:T(1,128)S(1)}, f32[1,256]{1,0:T(1,128)S(1)}, u32[]{:S(2)}, u32[]{:S(2)}) collective-permute-start(f32[1,256]{1,0:T(1,128)S(1)} %get-tuple-element.20), channel_id=1, source_target_pairs={{8,0},{16,8},{24,16},{0,24},{9,1},{17,9},{25,17},{1,25},{10,2},{18... | collective-permute-start | bytes 3080 | tf_op jit(solution)/shard_map/ppermute | solution.py:20
where the time goes:
time: 135 us
  starting transfers between devices  40.9 us (30%)
  blocking collectives  40.5 us (30%)
  other arithmetic  18.6 us (14%)
  waiting for transfers between devices  17.3 us (13%)
  local copies, waits for them, and re-layouts  8.87 us (7%)
  between operations  8.46 us (6%)
    psum x1, blocking collectives, local(): lax.psum((jnp.sum(right_side * image), jnp.sum(image * image)), ('circ',...  40.5 us
    ppermute x6, starting transfers between devices, with_halo(): lax.ppermute(head, axis, [((i + 1) % count, i) for i in range(count)])  20.4 us
    ppermute x10, starting transfers between devices, shifted(): return lax.ppermute(block, axis, route)  17.4 us
    ppermute x10, waiting for transfers between devices, shifted(): return lax.ppermute(block, axis, route)  11.6 us
    scatter-add x2, other arithmetic, give_back(): collect = collect.at[after_idx].add((1.0 - weight) * response)  7.24 us
    scatter-add x2, other arithmetic, give_back(): collect = collect.at[local_idx].add(weight * response)  7.09 us
    gather x4, local copies, waits for them, and re-layouts, project(): return weight * window[local_idx] + (1.0 - weight) * window[after_idx]  6.29 us
    ppermute x6, waiting for transfers between devices, with_halo(): lax.ppermute(tail, axis, [(i, (i + 1) % count) for i in range(count)])  5.71 us
  transfers between devices with their start and end apart: 22, of which 7 were waited for; matrix products, arithmetic and copies ran while one was open for 4% of the time, Pallas kernels for 0%

commit v1 on v0

v1 whole, which is shorter than its diff:
```python
import functools

import jax
import jax.numpy as jnp
from jax import lax
from jax.experimental import pallas as pl
from jax.experimental.pallas import tpu as pltpu
from jax.sharding import PartitionSpec as P

W = 256
REACH = 3
SLIDE = 1280

LANES = 128
SUB = 8
SPAN = 2 * (REACH + 1)
HALO = 2 * SPAN
TAPS = range(-REACH, REACH + 2)
VMEM = pl.BlockSpec(memory_space=pltpu.VMEM)
PARAMS = pltpu.CompilerParams(vmem_limit_bytes=40 << 20)


def shifted(block, distance):
    count = lax.axis_size("circ")
    route = [((i - distance) % count, i) for i in range(count)]
    return lax.ppermute(block, "circ", route)


def up8(count):
    return -(-count // SUB) * SUB


def chunk_of(rows, most=136):
    return max(c for c in range(SUB, most + 1, SUB) if rows % c == 0)


def for_chunks(first, rows, body, init=None):
    step = chunk_of(rows)

    def one(i, carry):
        return body(pl.multiple_of(first + i * step, SUB), step, carry)

    return lax.fori_loop(0, rows // step, one, 0 if init is None else init)


def beside(parts):
    lane = lax.broadcasted_iota(jnp.int32, parts[0].shape, 1)
    ahead = [pltpu.roll(v, 1, 1) for v in parts]
    after = [pltpu.roll(v, LANES - 1, 1) for v in parts]
    out = []
    for h in range(len(parts)):
        before = ahead[h - 1] if h else jnp.zeros_like(parts[0])
        behind = after[h + 1] if h + 1 < len(parts) else jnp.zeros_like(parts[0])
        out.append(
            jnp.where(lane == 0, before, ahead[h])
            + jnp.where(lane == LANES - 1, behind, after[h])
        )
    return out


def around(field, at, rows, groups):
    mid = [field[h, pl.ds(at + SUB, rows), :] for h in range(groups)]
    side = beside(mid)
    total = [
        side[h] + field[h, pl.ds(at + SUB - 1, rows), :] + field[h, pl.ds(at + SUB + 1, rows), :]
        for h in range(groups)
    ]
    return mid, total


def gather_taps(taps, field, at, rows, groups):
    acc = [None] * groups
    for j, k in enumerate(TAPS):
        tap = taps[j, pl.ds(at + SUB, rows), :]
        for h in range(groups):
            term = tap * field[h, pl.ds(at + SUB + k, rows), :]
            acc[h] = term if acc[h] is None else acc[h] + term
    return acc


def return_taps(taps, field, at, rows, groups, acc):
    acc = list(acc)
    for j, k in enumerate(TAPS):
        tap = taps[j, pl.ds(at + SUB - k, rows), :]
        for h in range(groups):
            acc[h] = acc[h] + tap * field[h, pl.ds(at + SUB - k, rows), :]
    return acc


def before_kernel(rows, groups, plan, b, cr, prev, nxt, *refs):
    pieces, (taps, bs, crs, proj, base, scratch, share, offs) = refs[: len(plan)], refs[len(plan) :]
    frame = rows + 2 * HALO
    edge = jnp.zeros((SUB, LANES), jnp.float32)
    for h in range(groups):
        lanes = slice(h * LANES, (h + 1) * LANES)
        bs[h, 0:SUB, :] = edge
        bs[h, SUB : SUB + HALO, :] = prev[0:HALO, lanes]
        bs[h, SUB + HALO : SUB + HALO + rows, :] = b[:, lanes]
        bs[h, SUB + HALO + rows : SUB + frame, :] = nxt[0:HALO, lanes]
        bs[h, SUB + frame :, :] = edge
        for lo, hi in ((0, HALO - SPAN), (frame - HALO + SPAN, frame)):
            crs[h, lo:hi, :] = jnp.zeros((hi - lo, LANES), jnp.float32)
        crs[h, HALO - SPAN : HALO, :] = prev[HALO : HALO + SPAN, lanes]
        crs[h, HALO : HALO + rows, :] = cr[:, lanes]
        crs[h, HALO + rows : HALO + rows + SPAN, :] = nxt[HALO : HALO + SPAN, lanes]
        for field in (proj, scratch):
            field[h, 0:SUB, :] = edge
            field[h, SUB + frame :, :] = edge
    for piece, (first, length, row) in zip(pieces, plan, strict=True):
        width = groups * LANES
        lines = -(-length // width)
        for target, line in ((share, row), (offs, row + lines)):
            for start in range(0, length, LANES):
                count = min(LANES, length - start)
                r, c = line + start // width, start % width
                square = jnp.broadcast_to(piece[r : r + 1, c : c + LANES], (LANES, LANES)).T
                target[first + start : first + start + count, :] = square[:count]
    for j in range(len(TAPS)):
        taps[j, 0:SUB, :] = edge
        taps[j, SUB + frame :, :] = edge

    def fill(at, step, carry):
        part = share[pl.ds(at, step), :]
        rest = 1.0 - part
        off = offs[pl.ds(at, step), :]
        for j, k in enumerate(TAPS):
            taps[j, pl.ds(at + SUB, step), :] = jnp.where(
                off == k, part, jnp.where(off == k - 1, rest, 0.0)
            )
        return carry

    for_chunks(0, frame, fill)

    def project(at, step, carry):
        acc = gather_taps(taps, bs, at, step, groups)
        for h in range(groups):
            proj[h, pl.ds(at + SUB, step), :] = acc[h]
        return carry

    for_chunks(0, frame, project)

    def neighbours(at, step, carry):
        _, total = around(proj, at, step, groups)
        for h in range(groups):
            scratch[h, pl.ds(at + SUB, step), :] = -0.25 * total[h]
        return carry

    for_chunks(0, frame, neighbours)

    def start(at, step, carry):
        mid, total = around(bs, at, step, groups)
        acc = [crs[h, pl.ds(at, step), :] * mid[h] - 0.25 * total[h] for h in range(groups)]
        acc = return_taps(taps, scratch, at, step, groups, acc)
        for h in range(groups):
            base[h, pl.ds(at, step), :] = acc[h]
        return carry

    for_chunks(0, frame, start)


def apply_kernel(rows, groups, devices, plan, taps, bs, crs, proj, base, *refs):
    pieces = refs[: len(plan)]
    image, second, sums, resp, cs, proj_two = refs[len(plan) :]
    frame = rows + 2 * HALO
    edge = jnp.zeros((SUB, LANES), jnp.float32)
    for h in range(groups):
        lanes = slice(h * LANES, (h + 1) * LANES)
        for piece, (first, length, _) in zip(pieces, plan, strict=True):
            cs[h, first : first + length, :] = piece[:, lanes]
        for field in (image, resp, proj_two):
            field[h, 0:SUB, :] = edge
            field[h, SUB + frame :, :] = edge

    def scale(at, step, carry):
        for h in range(groups):
            resp[h, pl.ds(at + SUB, step), :] = (
                cs[h, pl.ds(at, step), :] * proj[h, pl.ds(at + SUB, step), :]
            )
        return carry

    for_chunks(0, frame, scale)

    def first(at, step, carry):
        acc = [base[h, pl.ds(at, step), :] for h in range(groups)]
        acc = return_taps(taps, resp, at, step, groups, acc)
        for h in range(groups):
            image[h, pl.ds(at + SUB, step), :] = acc[h]
        return carry

    for_chunks(0, frame, first)

    def project(at, step, carry):
        acc = gather_taps(taps, image, at, step, groups)
        for h in range(groups):
            proj_two[h, pl.ds(at + SUB, step), :] = acc[h]
        return carry

    for_chunks(0, frame, project)

    def respond(at, step, carry):
        mid, total = around(proj_two, at, step, groups)
        for h in range(groups):
            resp[h, pl.ds(at + SUB, step), :] = (
                cs[h, pl.ds(at, step), :] * mid[h] - 0.25 * total[h]
            )
        return carry

    for_chunks(0, frame, respond)

    def last(at, step, carry):
        mid, total = around(image, at, step, groups)
        acc = [crs[h, pl.ds(at, step), :] * mid[h] - 0.25 * total[h] for h in range(groups)]
        acc = return_taps(taps, resp, at, step, groups, acc)
        carry = list(carry)
        for h in range(groups):
            second[h, pl.ds(at - HALO, step), :] = acc[h]
            right = bs[h, pl.ds(at + SUB, step), :]
            pairs = ((right, mid[h]), (right, acc[h]), (mid[h], mid[h]), (mid[h], acc[h]), (acc[h], acc[h]))
            for j, (u, v) in enumerate(pairs):
                carry[j] = carry[j] + jnp.sum((u * v).reshape(step // SUB, SUB, LANES), axis=0)
        return tuple(carry)

    totals = for_chunks(HALO, rows, last, tuple(jnp.zeros((SUB, LANES), jnp.float32) for _ in range(5)))
    lane = lax.broadcasted_iota(jnp.int32, (SUB, LANES), 1)
    line = jnp.zeros((SUB, LANES), jnp.float32)
    for j, total in enumerate(totals):
        line = jnp.where(lane == j, jnp.sum(total), line)
    sums[...] = jnp.broadcast_to(line[0:1], (devices, LANES))


def finish_kernel(rows, groups, parts, bs, image, second, solution_out, residual_out, sol, res, sems):
    total = jnp.sum(parts[...], axis=0, keepdims=True)
    b_p, b_q, p_p, p_q, q_q = (total[:, j : j + 1] for j in range(5))
    det = p_p * q_q - p_q * p_q
    y1 = (q_q * b_p - p_q * b_q) / det
    y2 = (p_p * b_q - p_q * b_p) / det
    step = chunk_of(rows, 128)
    copies = []
    for i in range(rows // step):
        at = i * step
        one = jnp.broadcast_to(y1, (step, LANES))
        two = jnp.broadcast_to(y2, (step, LANES))
        for h in range(groups):
            lanes = slice(h * LANES, (h + 1) * LANES)
            b = bs[h, at + SUB + HALO : at + SUB + HALO + step, :]
            p = image[h, at + SUB + HALO : at + SUB + HALO + step, :]
            q = second[h, at : at + step, :]
            sol[at : at + step, lanes] = one * b + two * p
            res[at : at + step, lanes] = b - one * p - two * q
        for j, (src, dst) in enumerate(((sol, solution_out), (res, residual_out))):
            copy = pltpu.make_async_copy(
                src.at[pl.ds(at, step)], dst.at[pl.ds(at, step)], sems.at[i, j]
            )
            copy.start()
            copies.append(copy)
    for copy in copies:
        copy.wait()


def local(right_side, coef_rotor, coef_stator, mortar_rows, mortar_weight):
    rows, cols = right_side.shape
    groups = cols // LANES
    count = lax.axis_size("circ")
    devices = count * lax.axis_size("radax")
    total_rows = rows * count
    frame = rows + 2 * HALO
    whole, remainder = divmod(SLIDE, rows)
    assert cols == W and rows % SUB == 0 and remainder % SUB == 0
    assert HALO <= remainder <= rows - HALO

    stator = lax.axis_index("circ") * rows + jnp.arange(rows, dtype=jnp.int32)
    offset = jnp.mod(mortar_rows - stator - SLIDE + total_rows // 2, total_rows) - total_rows // 2
    offset = offset.astype(jnp.float32)
    routes = [(whole + 1, rows - remainder - HALO, rows), (whole, 0, rows - remainder + HALO)]
    coefs = [shifted(coef_stator[lo:hi], by) for by, lo, hi in routes]

    mail = {}

    def post(by, block):
        blocks = mail.setdefault(by % count, [])
        at = sum(x.shape[0] for x in blocks)
        blocks.append(jnp.pad(block, ((0, up8(block.shape[0]) - block.shape[0]), (0, 0))))
        return by % count, at, block.shape[0]

    def in_lines(vector):
        lines = -(-vector.shape[0] // cols)
        return jnp.pad(vector, (0, lines * cols - vector.shape[0])).reshape(lines, cols)

    tags = [
        post(1, jnp.concatenate([right_side[rows - HALO :], coef_rotor[rows - SPAN :]])),
        post(-1, jnp.concatenate([right_side[:HALO], coef_rotor[:SPAN]])),
    ]
    for by, lo, hi in routes:
        tags.append(post(by, jnp.concatenate([in_lines(mortar_weight[lo:hi]), in_lines(offset[lo:hi])])))
    arrived = {by: shifted(jnp.concatenate(blocks), by) for by, blocks in mail.items()}
    prev, nxt, *pieces = [arrived[by][at : at + up8(size)] for by, at, size in tags]

    plan, first = [], 0
    for _, lo, hi in routes:
        plan.append((first, hi - lo, 0))
        first += hi - lo

    def vmem(*shape):
        return pltpu.VMEM(shape, jnp.float32)

    held = rows + 2 * HALO + 2 * SUB
    taps, bs, crs, proj, base = pl.pallas_call(
        functools.partial(before_kernel, rows, groups, plan),
        out_shape=[
            vmem(len(TAPS), held, LANES),
            vmem(groups, held, LANES),
            vmem(groups, frame, LANES),
            vmem(groups, held, LANES),
            vmem(groups, frame, LANES),
        ],
        in_specs=[VMEM] * (4 + len(pieces)),
        out_specs=[VMEM] * 5,
        scratch_shapes=[vmem(groups, held, LANES), vmem(frame, LANES), vmem(frame, LANES)],
        compiler_params=PARAMS,
        name="before",
    )(right_side, coef_rotor, prev, nxt, *pieces)

    image, second, sums = pl.pallas_call(
        functools.partial(apply_kernel, rows, groups, devices, plan),
        out_shape=[
            vmem(groups, held, LANES),
            vmem(groups, rows, LANES),
            vmem(devices, LANES),
        ],
        in_specs=[VMEM] * (5 + len(coefs)),
        out_specs=[VMEM] * 3,
        scratch_shapes=[vmem(groups, held, LANES), vmem(groups, frame, LANES), vmem(groups, held, LANES)],
        compiler_params=PARAMS,
        name="apply",
    )(taps, bs, crs, proj, base, *coefs)

    parts = lax.all_to_all(sums, ("circ", "radax"), 0, 0, tiled=True)

    step = chunk_of(rows, 128)
    return pl.pallas_call(
        functools.partial(finish_kernel, rows, groups),
        out_shape=[jax.ShapeDtypeStruct((rows, cols), jnp.float32)] * 2,
        in_specs=[VMEM] * 4,
        out_specs=[pl.BlockSpec(memory_space=pl.ANY)] * 2,
        scratch_shapes=[
            vmem(rows, cols),
            vmem(rows, cols),
            pltpu.SemaphoreType.DMA((rows // step, 2)),
        ],
        compiler_params=PARAMS,
        name="finish",
    )(parts, bs, image, second)


def solution(mesh):
    return jax.shard_map(
        local,
        mesh=mesh,
        in_specs=(P("circ", "radax"), P("circ", "radax"), P("circ", "radax"), P("circ"), P("circ")),
        out_specs=(P("circ", "radax"), P("circ", "radax")),
        check_vma=False,
    )
```

time: 135 us -> 48 us (0.36)
  starting transfers between devices: 40.9 us -> 9.39 us
  blocking collectives: 40.5 us -> 12.7 us
  other arithmetic: 18.6 us -> 1.47 us
  between operations: 8.46 us -> 0.69 us
  Pallas kernels: 0 us -> 6.62 us
  waiting for transfers between devices: 17.3 us -> 11.8 us
  local copies, waits for them, and re-layouts: 8.87 us -> 4.8 us
    psum x1 -> x0, blocking collectives: 40.5 us -> none  [local(): lax.psum((jnp.sum(right_side * image), jnp.sum(image * image)), ('circ',...]
    ppermute x22 -> x5, starting transfers between devices: 40.9 us -> 9.39 us  [shifted(): return lax.ppermute(block, 'circ', route)]
    scatter-add x4 -> x0, other arithmetic: 14.3 us -> none  [the longest x2 7.24 us: give_back(): collect = collect.at[after_idx].add((1.0 - weight) * response)]
    all_to_all x0 -> x1, blocking collectives: none -> 12.7 us  [local(): parts = lax.all_to_all(sums, ('circ', 'radax'), 0, 0, tiled=True)]
    pallas_call x0 -> x3, Pallas kernels: none -> 6.62 us  [the longest x1 2.67 us: local(): pl.pallas_call(functools.partial(before_kernel, rows, groups, plan), out_...]
    gather x4 -> x0, local copies, waits for them, and re-layouts: 6.29 us -> none  [project(): return weight * window[local_idx] + (1.0 - weight) * window[after_idx]]
    ppermute x22 -> x5, waiting for transfers between devices: 17.3 us -> 11.8 us  [shifted(): return lax.ppermute(block, 'circ', route)]
    sub x4 -> x0, other arithmetic: 1.82 us -> none  [the longest x1 1.09 us: local(): residual = right_side - coeff_one * image - coeff_two * second]
  transfers between devices with their start and end apart: 22 -> 5, of which waited for: 7 -> 2; matrix products, arithmetic and copies ran while one was open for 4% -> 7% of each run, Pallas kernels for 0% -> 6%
where the time goes in v1:
time: 48 us; the launch traced here: 47.5 us
  blocking collectives  12.7 us (26%)
  waiting for transfers between devices  11.8 us (25%)
  starting transfers between devices  9.39 us (20%)
  Pallas kernels  6.62 us (14%)
  local copies, waits for them, and re-layouts  4.8 us (10%)
  other arithmetic  1.47 us (3%)
  between operations  0.69 us (1%)
    all_to_all x1, blocking collectives, local(): parts = lax.all_to_all(sums, ('circ', 'radax'), 0, 0, tiled=True)  12.7 us
    ppermute x5, waiting for transfers between devices, shifted(): return lax.ppermute(block, 'circ', route)  11.8 us
    ppermute x5, starting transfers between devices, shifted(): return lax.ppermute(block, 'circ', route)  9.39 us
    pallas_call x1, Pallas kernels, local(): pl.pallas_call(functools.partial(before_kernel, rows, groups, plan), out_...  2.67 us
    pallas_call x1, Pallas kernels, local(): pl.pallas_call(functools.partial(apply_kernel, rows, groups, devices, pla...  2.64 us
    unnamed x4, local copies, waits for them, and re-layouts  2.08 us
    pallas_call x1, Pallas kernels, local(): pl.pallas_call(functools.partial(finish_kernel, rows, groups), out_shape=...  1.31 us
    slice x1, local copies, waits for them, and re-layouts, local(): coefs = [shifted(coef_stator[lo:hi], by) for by, lo, hi in routes]  1.08 us
  transfers between devices with their start and end apart: 5, of which 2 were waited for; matrix products, arithmetic and copies ran while one was open for 7% of the time, Pallas kernels for 6%

profile of v1, /device:TPU:0, one launch (start us, length us, event | category | flops | bytes accessed | tf_op | source)
XLA Modules:
  0.0 47.5 jit_solution(11637869466244411109)
XLA Ops:
  0.6 1.1 %fusion.4 = (f32[272,256]{1,0:T(8,128)S(1)}, f32[272,256]{1,0:T(8,128)S(1)}) fusion(f32[512,256]{1,0:T(8,128)} %param.7), kind=kLoop, calls=%fused_computation.13 | loop fusion | bytes 1114112 | tf_op jit(solution)/shard_map/slice | solution.py:275
  1.7 4.1 %collective-permute-start.4 = (f32[272,256]{1,0:T(8,128)S(1)}, f32[272,256]{1,0:T(8,128)S(1)}, u32[]{:S(2)}, u32[]{:S(2)}) collective-permute-start(f32[272,256]{1,0:T(8,128)S(1)} %get-tuple-element.20), channel_id=1, source_target_pairs={{16,0},{24,8},{0,16},{8,24},{17,1},{25,9},{1,17},{9,25},{18,2},{26... | collective-permute-start | bytes 835592 | tf_op jit(solution)/shard_map/ppermute | solution.py:26
  5.8 1.3 %collective-permute-start.3 = (f32[272,256]{1,0:T(8,128)S(1)}, f32[272,256]{1,0:T(8,128)S(1)}, u32[]{:S(2)}, u32[]{:S(2)}) collective-permute-start(f32[272,256]{1,0:T(8,128)S(1)} %get-tuple-element.21), channel_id=1, source_target_pairs={{8,0},{16,8},{24,16},{0,24},{9,1},{17,9},{25,17},{1,25},{10,2},{18... | collective-permute-start | bytes 835592 | tf_op jit(solution)/shard_map/ppermute | solution.py:26
  7.2 0.8 %slice.40 = f32[272]{0:T(512)S(1)} slice(f32[512]{0:T(512)} %param.9), slice={[240:512]} | slice | bytes 2176 | tf_op jit(solution)/shard_map/slice | solution.py:294
  7.9 0.7 %broadcast_select_fusion = (f32[512]{0:T(512)S(1)}, f32[512]{0:T(512)S(1)}, f32[512]{0:T(512)S(1)}) fusion(pred[512]{0:T(512)(128)(4,1)} %constant.38.clone.1, s32[512]{0:T(512)} %param.8, s32[]{:T(128)S(6)} %mul.3, f32[512]{0:T(512)} %param.9), kind=kLoop, calls=%fused_computation.11 | loop fusion | flops 9216 | bytes 10756 | tf_op jit(solution)/shard_map/jit(_pad)/pad | solution.py:287
  8.7 0.1 slice.41
  8.8 0.7 %fusion.5 = (f32[16,256]{1,0:T(8,128)S(1)}, f32[16,256]{1,0:T(8,128)S(1)}) fusion(f32[512,256]{1,0:T(8,128)} %b.1), kind=kLoop, calls=%fused_computation.14 | loop fusion | bytes 65536 | tf_op jit(solution)/shard_map/slice | solution.py:291
  9.5 0.7 %fusion.6 = (f32[8,256]{1,0:T(8,128)S(1)}, f32[8,256]{1,0:T(8,128)S(1)}, f32[8,256]{1,0:T(8,128)S(1)}) fusion(f32[512,256]{1,0:T(8,128)} %cr.1, f32[2,256]{1,0:T(2,128)S(1)} %reshape.25, f32[2,256]{1,0:T(2,128)S(1)} %reshape.24), kind=kLoop, calls=%fused_computation.15 | loop fusion | flops 8192 | bytes 45056 | tf_op jit(solution)/shard_map/slice | solution.py:291
  10.2 0.7 %collective-permute-start = (f32[24,256]{1,0:T(8,128)S(1)}, f32[24,256]{1,0:T(8,128)S(1)}, u32[]{:S(2)}, u32[]{:S(2)}) collective-permute-start(f32[24,256]{1,0:T(8,128)S(1)} %pad_maximum_fusion.1), channel_id=1, source_target_pairs={{24,0},{0,8},{8,16},{16,24},{25,1},{1,9},{9,17},{17,25},{26,2},{2,... | collective-permute-start | bytes 73736 | tf_op jit(solution)/shard_map/ppermute | solution.py:26
  11.0 3.1 %collective-permute-start.1 = (f32[32,256]{1,0:T(8,128)S(1)}, f32[32,256]{1,0:T(8,128)S(1)}, u32[]{:S(2)}, u32[]{:S(2)}) collective-permute-start(f32[32,256]{1,0:T(8,128)S(1)} %pad_maximum_fusion), channel_id=1, source_target_pairs={{8,0},{16,8},{24,16},{0,24},{9,1},{17,9},{25,17},{1,25},{10,2},{18... | collective-permute-start | bytes 98312 | tf_op jit(solution)/shard_map/ppermute | solution.py:26
  14.2 0.1 collective-permute-start.2
  14.2 5.5 %collective-permute-done.1 = f32[32,256]{1,0:T(8,128)S(1)} collective-permute-done((f32[32,256]{1,0:T(8,128)S(1)}, f32[32,256]{1,0:T(8,128)S(1)}, u32[]{:S(2)}, u32[]{:S(2)}) %collective-permute-start.1) | collective-permute-done | bytes 32800 | tf_op jit(solution)/shard_map/ppermute | solution.py:26
  19.7 6.3 %collective-permute-done.2.refs_1_ = f32[8,256]{1,0:T(8,128)S(1)} collective-permute-done((f32[8,256]{1,0:T(8,128)S(1)}, f32[8,256]{1,0:T(8,128)S(1)}, u32[]{:S(2)}, u32[]{:S(2)}) %collective-permute-start.2) | collective-permute-done | bytes 8224 | tf_op jit(solution)/shard_map/ppermute | solution.py:26
  26.0 0.0 collective-permute-done.prev
  26.0 0.0 copy-start
  26.0 1.0 %copy-done = f32[512,256]{1,0:T(8,128)S(1)} copy-done((f32[512,256]{1,0:T(8,128)S(1)}, f32[512,256]{1,0:T(8,128)}, u32[]{:S(2)}) %copy-start) | copy-done | bytes 524312
  27.1 0.0 copy-start.1
  27.1 1.0 %copy-done.1 = f32[512,256]{1,0:T(8,128)S(1)} copy-done((f32[512,256]{1,0:T(8,128)S(1)}, f32[512,256]{1,0:T(8,128)}, u32[]{:S(2)}) %copy-start.1) | copy-done | bytes 524312
  28.1 2.7 %before.1 = (f32[8,560,128]{2,1,0:T(8,128)S(1)}, f32[2,560,128]{2,1,0:T(8,128)S(1)}, f32[2,544,128]{2,1,0:T(8,128)S(1)}, f32[2,560,128]{2,1,0:T(8,128)S(1)}, f32[2,544,128]{2,1,0:T(8,128)S(1)}) custom-call(f32[512,256]{1,0:T(8,128)S(1)} %copy-done, f32[512,256]{1,0:T(8,128)S(1)} %copy-done.1, f32[24,256]{1,0:T(8,128)S(1)} %collective-permute-done.prev, ...), custom_call_target="tpu_custom_call" | custom-call | tf_op jit(solution)/shard_map/before/pallas_call | solution.py:307
  30.8 0.0 collective-permute-done.4.refs_1_
  30.8 0.0 collective-permute-done.3.refs_0_
  30.8 2.6 %apply.1 = (f32[2,560,128]{2,1,0:T(8,128)S(1)}, f32[2,512,128]{2,1,0:T(8,128)S(1)}, f32[32,128]{1,0:T(8,128)S(1)}) custom-call(f32[8,560,128]{2,1,0:T(8,128)S(1)} %get-tuple-element.10.taps, f32[2,560,128]{2,1,0:T(8,128)S(1)} %get-tuple-element.11.bs, f32[2,544,128]{2,1,0:T(8,128)S(1)} %get-tuple-element.12.crs, f32[2,560,128]{2,1,0:T(8,128)S(1)} %get-tuple-element.13.proj, ...), custom_call_target="tpu_custom_call" | custom-call | tf_op jit(solution)/shard_map/apply/pallas_call | solution.py:323
  33.5 12.7 %all_to_all.11 = f32[32,1,128]{2,1,0:T(1,128)S(1)} all-to-all(f32[32,1,128]{2,1,0:T(1,128)S(1)} %bitcast.5), channel_id=1, replica_groups=mesh['circ'=4,'radax'=8] {'circ','radax'}, dimensions={0} | all-to-all | bytes 32768 | tf_op jit(solution)/shard_map/all_to_all | solution.py:337
  46.2 1.3 %finish.1 = (f32[512,256]{1,0:T(8,128)}, f32[512,256]{1,0:T(8,128)}) custom-call(f32[32,128]{1,0:T(8,128)S(1)} %bitcast.4, f32[2,560,128]{2,1,0:T(8,128)S(1)} %get-tuple-element.11.bs, f32[2,560,128]{2,1,0:T(8,128)S(1)} %get-tuple-element.16.image, f32[2,512,128]{2,1,0:T(8,128)S(1)} %get-tuple-element.17.second), custom_call_target="tpu_custom_call" | custom-call | tf_op jit(solution)/shard_map/finish/pallas_call | solution.py:340
  (11 shorter events, 0.1 us)
Async XLA Ops:
  1.7 29.1 %collective-permute-start.4 = (f32[272,256]{1,0:T(8,128)S(1)}, f32[272,256]{1,0:T(8,128)S(1)}, u32[]{:S(2)}, u32[]{:S(2)}) collective-permute-start(f32[272,256]{1,0:T(8,128)S(1)} %get-tuple-element.20), channel_id=1, source_target_pairs={{16,0},{24,8},{0,16},{8,24},{17,1},{25,9},{1,17},{9,25},{18,2},{26... | collective-permute-start | bytes 835592 | tf_op jit(solution)/shard_map/ppermute | solution.py:26
  5.8 25.0 %collective-permute-start.3 = (f32[272,256]{1,0:T(8,128)S(1)}, f32[272,256]{1,0:T(8,128)S(1)}, u32[]{:S(2)}, u32[]{:S(2)}) collective-permute-start(f32[272,256]{1,0:T(8,128)S(1)} %get-tuple-element.21), channel_id=1, source_target_pairs={{8,0},{16,8},{24,16},{0,24},{9,1},{17,9},{25,17},{1,25},{10,2},{18... | collective-permute-start | bytes 835592 | tf_op jit(solution)/shard_map/ppermute | solution.py:26
  10.2 15.8 %collective-permute-start = (f32[24,256]{1,0:T(8,128)S(1)}, f32[24,256]{1,0:T(8,128)S(1)}, u32[]{:S(2)}, u32[]{:S(2)}) collective-permute-start(f32[24,256]{1,0:T(8,128)S(1)} %pad_maximum_fusion.1), channel_id=1, source_target_pairs={{24,0},{0,8},{8,16},{16,24},{25,1},{1,9},{9,17},{17,25},{26,2},{2,... | collective-permute-start | bytes 73736 | tf_op jit(solution)/shard_map/ppermute | solution.py:26
  11.0 8.7 %collective-permute-start.1 = (f32[32,256]{1,0:T(8,128)S(1)}, f32[32,256]{1,0:T(8,128)S(1)}, u32[]{:S(2)}, u32[]{:S(2)}) collective-permute-start(f32[32,256]{1,0:T(8,128)S(1)} %pad_maximum_fusion), channel_id=1, source_target_pairs={{8,0},{16,8},{24,16},{0,24},{9,1},{17,9},{25,17},{1,25},{10,2},{18... | collective-permute-start | bytes 98312 | tf_op jit(solution)/shard_map/ppermute | solution.py:26
  14.2 11.9 %collective-permute-start.2 = (f32[8,256]{1,0:T(8,128)S(1)}, f32[8,256]{1,0:T(8,128)S(1)}, u32[]{:S(2)}, u32[]{:S(2)}) collective-permute-start(f32[8,256]{1,0:T(8,128)S(1)} %select_maximum_fusion), channel_id=1, source_target_pairs={{16,0},{24,8},{0,16},{8,24},{17,1},{25,9},{1,17},{9,25},{18,2},{26... | collective-permute-start | bytes 24584 | tf_op jit(solution)/shard_map/ppermute | solution.py:26
  26.0 1.0 %copy-start = (f32[512,256]{1,0:T(8,128)S(1)}, f32[512,256]{1,0:T(8,128)}, u32[]{:S(2)}) copy-start(f32[512,256]{1,0:T(8,128)} %b.1) | copy-start | bytes 1572868
  27.1 1.0 %copy-start.1 = (f32[512,256]{1,0:T(8,128)S(1)}, f32[512,256]{1,0:T(8,128)}, u32[]{:S(2)}) copy-start(f32[512,256]{1,0:T(8,128)} %cr.1) | copy-start | bytes 1572868

commit v2 on v0

v2 whole, which is shorter than its diff:
```python
import functools

import jax
import jax.numpy as jnp
import numpy as np
from jax import lax
from jax.experimental import pallas as pl
from jax.experimental.pallas import tpu as pltpu
from jax.sharding import PartitionSpec as P

W = 256
REACH = 3
SLIDE = 1280

LANES = 128
SUB = 8
SPAN = 2 * (REACH + 1)
HALO = 2 * SPAN
TAPS = range(-REACH, REACH + 2)
CHUNK = 64
LATER = (1, 3)
VMEM = pl.BlockSpec(memory_space=pltpu.VMEM)
PARAMS = pltpu.CompilerParams(vmem_limit_bytes=40 << 20)


def up8(count):
    return -(-count // SUB) * SUB


def vmem(*shape):
    return pltpu.VMEM(shape, jnp.float32)


def shifted(block, distance):
    count = lax.axis_size("circ")
    route = [((i - distance) % count, i) for i in range(count)]
    return lax.ppermute(block, "circ", route)


def near(mask, low, high):
    out = np.ones_like(mask)
    for k in range(low, high + 1):
        moved = np.zeros_like(mask)
        moved[max(0, -k) : len(mask) - max(0, k)] = mask[max(0, k) : len(mask) - max(0, -k)]
        out &= moved
    return out


def spread(mask, low, high):
    return ~near(~mask, -high, -low)


STAGES = ("proj", "resp", "image", "proj_two", "resp_two", "second")


def reachable(own, trace, coef, tap):
    proj = tap & near(trace, TAPS[0], TAPS[-1])
    resp = coef & near(proj, -1, 1)
    image = trace & near(trace, -1, 1) & near(resp & tap, -TAPS[-1], -TAPS[0])
    proj_two = tap & near(image, TAPS[0], TAPS[-1])
    resp_two = coef & near(proj_two, -1, 1)
    second = own & near(image, -1, 1) & near(resp_two & tap, -TAPS[-1], -TAPS[0])
    return dict(zip(STAGES, (proj, resp, image, proj_two, resp_two, second), strict=True))


def needed(own):
    resp_two = spread(own, -TAPS[-1], -TAPS[0])
    proj_two = spread(resp_two, -1, 1)
    image = spread(own, -1, 1) | spread(proj_two, TAPS[0], TAPS[-1])
    resp = spread(image, -TAPS[-1], -TAPS[0])
    proj = spread(resp, -1, 1)
    return dict(zip(STAGES, (proj, resp, image, proj_two, resp_two, own), strict=True))


def spans(mask, whole):
    tiles = mask.reshape(-1, SUB)
    tiles = tiles.all(1) if whole else tiles.any(1)
    edges = np.flatnonzero(np.diff(np.concatenate([[0], tiles.astype(np.int8), [0]])))
    return [(int(a) * SUB, int(b) * SUB) for a, b in zip(edges[::2], edges[1::2], strict=True)]


def for_chunks(ranges, body, carry=None):
    for first, last in ranges:
        for at in range(first, last, CHUNK):
            carry = body(at, min(CHUNK, last - at), carry)
    return carry


def beside(parts):
    lane = lax.broadcasted_iota(jnp.int32, parts[0].shape, 1)
    ahead = [pltpu.roll(v, 1, 1) for v in parts]
    after = [pltpu.roll(v, LANES - 1, 1) for v in parts]
    out = []
    for h in range(len(parts)):
        before = ahead[h - 1] if h else jnp.zeros_like(parts[0])
        behind = after[h + 1] if h + 1 < len(parts) else jnp.zeros_like(parts[0])
        out.append(
            jnp.where(lane == 0, before, ahead[h])
            + jnp.where(lane == LANES - 1, behind, after[h])
        )
    return out


def around(field, at, step):
    groups = field.shape[0]
    at += SUB
    mid = [field[h, at : at + step, :] for h in range(groups)]
    side = beside(mid)
    total = [
        side[h] + field[h, at - 1 : at - 1 + step, :] + field[h, at + 1 : at + 1 + step, :]
        for h in range(groups)
    ]
    return mid, total


def project(taps, field, at, step):
    acc = [None] * field.shape[0]
    at += SUB
    for j, k in enumerate(TAPS):
        tap = taps[j, at : at + step, :]
        for h in range(len(acc)):
            term = tap * field[h, at + k : at + k + step, :]
            acc[h] = term if acc[h] is None else acc[h] + term
    return acc


def give_back(taps, field, at, step, acc):
    acc = list(acc)
    at += SUB
    for j, k in enumerate(TAPS):
        tap = taps[j, at - k : at - k + step, :]
        for h in range(len(acc)):
            acc[h] = acc[h] + tap * field[h, at - k : at - k + step, :]
    return acc


def pack_kernel(rows, total_rows, messages, b, cr, cs, mortar, weight, *refs):
    outs, (mortar_here, weight_here, lines, sems) = refs[: len(messages)], refs[len(messages) :]
    sources = {"trace": b, "rotor": cr, "stator": cs}
    small = [
        pltpu.make_async_copy(mortar, mortar_here, sems.at[-1 + sems.shape[0]]),
        pltpu.make_async_copy(weight, weight_here, sems.at[-2 + sems.shape[0]]),
    ]
    for copy in small:
        copy.start()
    copies = []
    for out, (_, parts) in zip(outs, messages, strict=True):
        for kind, row, what in parts:
            if kind == "lines":
                continue
            for source, low, size, skip in what:
                copy = pltpu.make_async_copy(
                    sources[source].at[pl.ds(low, size)], out.at[pl.ds(row + skip, size)], sems.at[len(copies)]
                )
                copy.start()
                copies.append(copy)
    for copy in small:
        copy.wait()
    count = rows // LANES
    shape = (count, LANES)
    facing = lax.rem(lax.axis_index("circ") * rows + SLIDE, total_rows)
    facing = (
        facing
        + lax.broadcasted_iota(jnp.int32, shape, 0) * LANES
        + lax.broadcasted_iota(jnp.int32, shape, 1)
    )
    offset = mortar_here[...] - jnp.where(facing >= total_rows, facing - total_rows, facing)
    offset = jnp.where(offset > total_rows // 2, offset - total_rows, offset)
    offset = jnp.where(offset < -(total_rows // 2), offset + total_rows, offset)
    lines[:, 0:LANES] = weight_here[...]
    lines[:, LANES : 2 * LANES] = offset.astype(jnp.float32)
    for copy in copies:
        copy.wait()
    for out, (_, parts) in zip(outs, messages, strict=True):
        for kind, row, _ in parts:
            if kind == "lines":
                out[row : row + count, :] = lines[...]


STATE = ("trace", "coef", "taps", *STAGES, "sums")


def step_kernel(rows, opening, closing, work, fills, coefs, count, *refs):
    refs = list(refs)
    mail = refs[:count]
    refs = refs[count:]
    if work["starts"]:
        own, own_coef = refs[:2]
        refs = refs[2:]
    else:
        refs = refs[len(STATE) :]
    state = dict(zip(STATE, refs, strict=False))
    rest = refs[len(STATE) :]
    trace, coef, taps = state["trace"], state["coef"], state["taps"]
    groups = trace.shape[0]
    frame = rows + 2 * HALO

    for h in range(groups):
        lanes = slice(h * LANES, (h + 1) * LANES)
        if work["starts"]:
            trace[h, SUB + HALO : SUB + HALO + rows, :] = own[:, lanes]
            coef[h, HALO : HALO + rows, :] = own_coef[:, lanes]
        for edge, m, row in opening:
            at = 0 if edge == "head" else HALO + rows
            trace[h, SUB + at : SUB + at + HALO, :] = mail[m][row : row + HALO, lanes]
            at = HALO - SPAN if edge == "head" else HALO + rows
            coef[h, at : at + SPAN, :] = mail[m][row + HALO : row + HALO + SPAN, lanes]

    share, offs = rest[-2:]
    for m, row, low, high, first in fills:
        for line in range(low // LANES, -(-high // LANES)):
            a, b = max(low, line * LANES), min(high, (line + 1) * LANES)
            at, skip, size = first + a - low, a - line * LANES, b - a
            for target, lane in ((share, 0), (offs, LANES)):
                values = mail[m][row + line : row + line + 1, lane : lane + LANES]
                square = jnp.broadcast_to(values, (LANES, LANES)).T
                target[at : at + size, :] = square[skip : skip + size]

        def fill(at, step, carry):
            part, off = share[at : at + step, :], offs[at : at + step, :]
            for j, k in enumerate(TAPS):
                taps[j, at + SUB : at + SUB + step, :] = jnp.where(
                    off == k, part, jnp.where(off == k - 1, 1.0 - part, 0.0)
                )
            return carry

        for_chunks([(first, first + high - low)], fill)

    def plain_project(source, target):
        def body(at, step, carry):
            for h, value in enumerate(project(taps, source, at, step)):
                target[h, at + SUB : at + SUB + step, :] = value
            return carry

        return body

    def respond(source, target, ranges):
        for m, row, first, end in coefs:
            def body(at, step, carry, m=m, row=row, first=first):
                mid, total = around(source, at, step)
                for h in range(groups):
                    scale = mail[m][row + at - first : row + at - first + step, h * LANES : (h + 1) * LANES]
                    target[h, at + SUB : at + SUB + step, :] = scale * mid[h] - 0.25 * total[h]
                return carry

            for_chunks([(max(a, first), min(b, end)) for a, b in ranges if max(a, first) < min(b, end)], body)

    def apply(source, response, at, step):
        mid, total = around(source, at, step)
        acc = [coef[h, at : at + step, :] * mid[h] - 0.25 * total[h] for h in range(groups)]
        return mid, give_back(taps, response, at, step, acc)

    def first_image(at, step, carry):
        for h, value in enumerate(apply(trace, state["resp"], at, step)[1]):
            state["image"][h, at + SUB : at + SUB + step, :] = value
        return carry

    def second_image(at, step, carry):
        mid, acc = apply(state["image"], state["resp_two"], at, step)
        carry = list(carry)
        for h in range(groups):
            state["second"][h, at - HALO : at - HALO + step, :] = acc[h]
            right = trace[h, at + SUB : at + SUB + step, :]
            pairs = ((right, mid[h]), (right, acc[h]), (mid[h], mid[h]), (mid[h], acc[h]), (acc[h], acc[h]))
            for j, (u, v) in enumerate(pairs):
                carry[j] = carry[j] + jnp.sum((u * v).reshape(step // SUB, SUB, LANES), axis=0)
        return carry

    for_chunks(work["proj"], plain_project(trace, state["proj"]))
    respond(state["proj"], state["resp"], work["resp"])
    for_chunks(work["image"], first_image)
    for_chunks(work["proj_two"], plain_project(state["image"], state["proj_two"]))
    respond(state["proj_two"], state["resp_two"], work["resp_two"])
    if work["starts"]:
        totals = [jnp.zeros((SUB, LANES), jnp.float32)] * 5
    else:
        totals = [state["sums"][j] for j in range(5)]
    totals = for_chunks(work["second"], second_image, totals)
    if closing:
        lane = lax.broadcasted_iota(jnp.int32, (SUB, LANES), 1)
        line = jnp.zeros((SUB, LANES), jnp.float32)
        for j, total in enumerate(totals):
            line = jnp.where(lane == j, jnp.sum(total), line)
        rest[0][...] = jnp.broadcast_to(line[0:1], rest[0].shape)
    else:
        for j, total in enumerate(totals):
            state["sums"][j] = total
    del frame


def finish_kernel(rows, groups, parts, trace, image, second, solution_out, residual_out, sol, res, sems):
    total = jnp.sum(parts[...], axis=0, keepdims=True)
    b_p, b_q, p_p, p_q, q_q = (total[:, j : j + 1] for j in range(5))
    det = p_p * q_q - p_q * p_q
    y1 = (q_q * b_p - p_q * b_q) / det
    y2 = (p_p * b_q - p_q * b_p) / det
    step = rows // 4
    copies = []
    for i in range(rows // step):
        at = i * step
        one = jnp.broadcast_to(y1, (step, LANES))
        two = jnp.broadcast_to(y2, (step, LANES))
        for h in range(groups):
            lanes = slice(h * LANES, (h + 1) * LANES)
            b = trace[h, at + SUB + HALO : at + SUB + HALO + step, :]
            p = image[h, at + SUB + HALO : at + SUB + HALO + step, :]
            q = second[h, at : at + step, :]
            sol[at : at + step, lanes] = one * b + two * p
            res[at : at + step, lanes] = b - one * p - two * q
        for j, (src, dst) in enumerate(((sol, solution_out), (res, residual_out))):
            copy = pltpu.make_async_copy(
                src.at[pl.ds(at, step)], dst.at[pl.ds(at, step)], sems.at[i, j]
            )
            copy.start()
            copies.append(copy)
    for copy in copies:
        copy.wait()


def local(right_side, coef_rotor, coef_stator, mortar_rows, mortar_weight):
    rows, cols = right_side.shape
    groups = cols // LANES
    count = lax.axis_size("circ")
    devices = count * lax.axis_size("radax")
    total_rows = rows * count
    frame = rows + 2 * HALO
    held = frame + 2 * SUB
    whole, remainder = divmod(SLIDE, rows)
    assert cols == W and rows % (4 * SUB) == 0 and remainder % SUB == 0
    assert HALO <= remainder <= rows - HALO

    assert rows % LANES == 0

    cut = remainder + HALO
    count_lines = rows // LANES
    spare = HALO - SPAN - REACH - 1
    assert count_lines <= spare
    later = frame - up8((frame - cut) * LATER[0] // LATER[1])
    below, above = whole + 1, whole

    def stator_rows(first, last, low):
        return ("coef", [("stator", first - low, last - first, 0)], first, last)

    low_below, low_above = cut - rows, cut
    edge = ("tail", [("trace", 0, HALO, 0), ("rotor", 0, SPAN, HALO)])
    start = ("head", [("trace", rows - HALO, HALO, 0), ("rotor", rows - SPAN, SPAN, HALO)])
    sent = [
        (below, [stator_rows(0, cut, low_below), ("lines", 0, rows - cut, rows, 0)]),
        (above, [stator_rows(cut, later, low_above), ("lines", None, 0, rows - cut + 2 * HALO, cut)]),
        (above, [stator_rows(later, frame, low_above)]),
        (1, [start]),
    ]
    if (below + 1) % count == 0:
        sent[0][1].append(edge)
    else:
        sent.append((-1, [edge]))
    messages, holds, heights = [], [], []
    for by, parts in sent:
        row, laid = 0, []
        for kind, what, *_ in parts:
            if kind == "lines" and what is not None:
                laid.append((kind, what, None))
                continue
            laid.append((kind, row, what))
            row += up8(count_lines if kind == "lines" else sum(size for _, _, size, _ in what))
        messages.append((by, laid))
        holds.append([(kind, at, rest) for (kind, at, _), (_, _, *rest) in zip(laid, parts, strict=True)])
        heights.append(row)
    copies = sum(len(what) for _, laid in messages for kind, _, what in laid if kind != "lines")
    packed = pl.pallas_call(
        functools.partial(pack_kernel, rows, total_rows, messages),
        out_shape=[vmem(height, cols) for height in heights],
        in_specs=[pl.BlockSpec(memory_space=pltpu.HBM)] * 5,
        out_specs=[VMEM] * len(messages),
        scratch_shapes=[
            pltpu.VMEM((count_lines, LANES), jnp.int32),
            vmem(count_lines, LANES),
            vmem(count_lines, cols),
            pltpu.SemaphoreType.DMA((copies + 2,)),
        ],
        compiler_params=PARAMS,
        name="pack",
    )(
        *(
            pltpu.with_memory_space_constraint(x, pltpu.HBM)
            for x in (
                right_side,
                coef_rotor,
                coef_stator,
                mortar_rows.reshape(count_lines, LANES),
                mortar_weight.reshape(count_lines, LANES),
            )
        )
    )
    arrived = [shifted(block, by) for block, (by, _) in zip(packed, messages, strict=True)]

    own = np.zeros(frame, bool)
    own[HALO : HALO + rows] = True
    known = {"trace": own.copy(), "coef": np.zeros(frame, bool), "taps": np.zeros(frame, bool)}
    done = {name: np.zeros(frame, bool) for name in STAGES}
    want = needed(own)
    coefs = []
    shapes = {name: vmem(groups, held, LANES) for name in STATE}
    shapes["coef"] = vmem(groups, frame, LANES)
    shapes["taps"] = vmem(len(TAPS), held, LANES)
    shapes["second"] = vmem(groups, rows, LANES)
    shapes["sums"] = vmem(5, SUB, LANES)

    steps = [[0], [1], list(range(2, len(sent)))]
    state, taken = None, []
    for number, batch in enumerate(steps):
        opening, fills = [], []
        for m in batch:
            taken.append(m)
            for kind, at, what in holds[m]:
                if kind in ("head", "tail"):
                    opening.append((kind, len(taken) - 1, at))
                    known["trace"][slice(0, HALO) if kind == "head" else slice(frame - HALO, frame)] = True
                elif kind == "lines":
                    low, high, first = what
                    fills.append((len(taken) - 1, at, low, high, first))
                    known["taps"][first : first + high - low] = True
                else:
                    first, last = what
                    coefs.append((len(taken) - 1, at, first, last))
                    known["coef"][max(first, spare) : last] = True
        can = reachable(own, known["trace"], known["coef"], known["taps"])
        work = {"starts": number == 0}
        for name in STAGES:
            whole_tiles = name == "second"
            work[name] = spans(can[name] & want[name] & ~done[name], whole_tiles)
            if whole_tiles:
                for a, b in work[name]:
                    done[name][a:b] = True
            else:
                done[name] |= can[name] & want[name]
        closing = number == len(steps) - 1
        out_shape = [shapes[name] for name in STATE] + [vmem(devices, LANES)] * closing
        inputs = [arrived[m] for m in taken]
        state = pl.pallas_call(
            functools.partial(
                step_kernel, rows, opening, closing, work, fills, list(coefs), len(taken)
            ),
            out_shape=out_shape,
            in_specs=[VMEM] * (len(taken) + (2 if number == 0 else len(STATE))),
            out_specs=[VMEM] * len(out_shape),
            scratch_shapes=[vmem(frame, LANES)] * 2,
            input_output_aliases={} if number == 0 else {len(taken) + i: i for i in range(len(STATE))},
            compiler_params=PARAMS,
            name=f"step{number}",
        )(*inputs, *([right_side, coef_rotor] if number == 0 else state))
    *state, line = state
    assert done["second"][HALO : HALO + rows].all()
    state = dict(zip(STATE, state, strict=True))

    parts = lax.all_to_all(line, ("circ", "radax"), 0, 0, tiled=True)

    return pl.pallas_call(
        functools.partial(finish_kernel, rows, groups),
        out_shape=[jax.ShapeDtypeStruct((rows, cols), jnp.float32)] * 2,
        in_specs=[VMEM] * 4,
        out_specs=[pl.BlockSpec(memory_space=pl.ANY)] * 2,
        scratch_shapes=[
            vmem(rows, cols),
            vmem(rows, cols),
            pltpu.SemaphoreType.DMA((4, 2)),
        ],
        compiler_params=PARAMS,
        name="finish",
    )(parts, state["trace"], state["image"], state["second"])


def solution(mesh):
    return jax.shard_map(
        local,
        mesh=mesh,
        in_specs=(P("circ", "radax"), P("circ", "radax"), P("circ", "radax"), P("circ"), P("circ")),
        out_specs=(P("circ", "radax"), P("circ", "radax")),
        check_vma=False,
    )
```

time: 135 us -> 41.1 us (0.30)
  starting transfers between devices: 40.9 us -> 8.03 us
  blocking collectives: 40.5 us -> 12.2 us
  other arithmetic: 18.6 us -> 0 us
  between operations: 8.46 us -> 0.68 us
  local copies, waits for them, and re-layouts: 8.87 us -> 2.08 us
  Pallas kernels: 0 us -> 6.63 us
  waiting for transfers between devices: 17.3 us -> 11.2 us
    psum x1 -> x0, blocking collectives: 40.5 us -> none  [local(): lax.psum((jnp.sum(right_side * image), jnp.sum(image * image)), ('circ',...]
    ppermute x22 -> x4, starting transfers between devices: 40.9 us -> 8.03 us  [shifted(): return lax.ppermute(block, 'circ', route)]
    scatter-add x4 -> x0, other arithmetic: 14.3 us -> none  [the longest x2 7.24 us: give_back(): collect = collect.at[after_idx].add((1.0 - weight) * response)]
    all_to_all x0 -> x1, blocking collectives: none -> 12.2 us  [local(): parts = lax.all_to_all(line, ('circ', 'radax'), 0, 0, tiled=True)]
    pallas_call x0 -> x5, Pallas kernels: none -> 6.63 us  [the longest x3 4.11 us: local(): pl.pallas_call(functools.partial(step_kernel, rows, opening, closing, wor...]
    gather x4 -> x0, local copies, waits for them, and re-layouts: 6.29 us -> none  [project(): return weight * window[local_idx] + (1.0 - weight) * window[after_idx]]
    ppermute x22 -> x4, waiting for transfers between devices: 17.3 us -> 11.2 us  [shifted(): return lax.ppermute(block, 'circ', route)]
    slice x11 -> x0, local copies, waits for them, and re-layouts: 1.82 us -> none  [the longest x1 1.06 us: local(): coef_stator[low_row:high_row]]
  transfers between devices with their start and end apart: 22 -> 4, of which waited for: 7 -> 2; matrix products, arithmetic and copies ran while one was open for 4% -> 0% of each run, Pallas kernels for 0% -> 8%
where the time goes in v2:
time: 41.1 us; the launch traced here: 40.9 us
  blocking collectives  12.2 us (30%)
  waiting for transfers between devices  11.2 us (27%)
  starting transfers between devices  8.03 us (20%)
  Pallas kernels  6.63 us (16%)
  local copies, waits for them, and re-layouts  2.08 us (5%)
  between operations  0.68 us (2%)
    all_to_all x1, blocking collectives, local(): parts = lax.all_to_all(line, ('circ', 'radax'), 0, 0, tiled=True)  12.2 us
    ppermute x4, waiting for transfers between devices, shifted(): return lax.ppermute(block, 'circ', route)  11.2 us
    ppermute x4, starting transfers between devices, shifted(): return lax.ppermute(block, 'circ', route)  8.03 us
    pallas_call x3, Pallas kernels, local(): pl.pallas_call(functools.partial(step_kernel, rows, opening, closing, wor...  4.11 us
    unnamed x4, local copies, waits for them, and re-layouts  2.08 us
    pallas_call x1, Pallas kernels, local(): pl.pallas_call(functools.partial(finish_kernel, rows, groups), out_shape=...  1.31 us
    pallas_call x1, Pallas kernels, local(): pl.pallas_call(functools.partial(pack_kernel, rows, total_rows, messages)...  1.21 us
  transfers between devices with their start and end apart: 4, of which 2 were waited for; matrix products, arithmetic and copies ran while one was open for 0% of the time, Pallas kernels for 8%

profile of v2, /device:TPU:0, one launch (start us, length us, event | category | flops | bytes accessed | tf_op | source)
XLA Modules:
  0.0 40.9 jit_solution(952916164276940900)
XLA Ops:
  0.6 1.2 %pack.1 = (f32[296,256]{1,0:T(8,128)S(1)}, f32[184,256]{1,0:T(8,128)S(1)}, f32[96,256]{1,0:T(8,128)S(1)}, f32[24,256]{1,0:T(8,128)S(1)}) custom-call(f32[512,256]{1,0:T(8,128)} %refs_1_.1, f32[512,256]{1,0:T(8,128)} %refs_2_.1, f32[512,256]{1,0:T(8,128)} %cs.1, s32[4,128]{1,0:T(4,128)} %bitcast.8, f32[4,128]{1,0:T(4,128)} %bitcast.9), custom_call_target="tpu_custom_call" | custom-call | tf_op jit(solution)/shard_map/pack/pallas_call | solution.py:370
  1.9 5.1 %collective-permute-start = (f32[296,256]{1,0:T(8,128)S(1)}, f32[296,256]{1,0:T(8,128)S(1)}, u32[]{:S(2)}, u32[]{:S(2)}) collective-permute-start(f32[296,256]{1,0:T(8,128)S(1)} %get-tuple-element.30), channel_id=1, source_target_pairs={{8,0},{16,8},{24,16},{0,24},{9,1},{17,9},{25,17},{1,25},{10,2},{18... | collective-permute-start | bytes 909320 | tf_op jit(solution)/shard_map/ppermute | solution.py:37
  7.0 0.0 collective-permute-start.1
  7.0 2.9 %collective-permute-start.2 = (f32[96,256]{1,0:T(8,128)S(1)}, f32[96,256]{1,0:T(8,128)S(1)}, u32[]{:S(2)}, u32[]{:S(2)}) collective-permute-start(f32[96,256]{1,0:T(8,128)S(1)} %get-tuple-element.32), channel_id=1, source_target_pairs={{16,0},{24,8},{0,16},{8,24},{17,1},{25,9},{1,17},{9,25},{18,2},{26... | collective-permute-start | bytes 294920 | tf_op jit(solution)/shard_map/ppermute | solution.py:37
  9.9 0.0 collective-permute-start.3
  9.9 4.7 %collective-permute-done.refs_0_ = f32[296,256]{1,0:T(8,128)S(1)} collective-permute-done((f32[296,256]{1,0:T(8,128)S(1)}, f32[296,256]{1,0:T(8,128)S(1)}, u32[]{:S(2)}, u32[]{:S(2)}) %collective-permute-start) | collective-permute-done | bytes 303136 | tf_op jit(solution)/shard_map/ppermute | solution.py:37
  14.6 0.0 copy-start
  14.6 1.0 %copy-done = f32[512,256]{1,0:T(8,128)S(1)} copy-done((f32[512,256]{1,0:T(8,128)S(1)}, f32[512,256]{1,0:T(8,128)}, u32[]{:S(2)}) %copy-start) | copy-done | bytes 524312
  15.6 0.0 copy-start.1
  15.6 1.0 %copy-done.1 = f32[512,256]{1,0:T(8,128)S(1)} copy-done((f32[512,256]{1,0:T(8,128)S(1)}, f32[512,256]{1,0:T(8,128)}, u32[]{:S(2)}) %copy-start.1) | copy-done | bytes 524312
  16.7 1.9 %step0.1 = (f32[2,560,128]{2,1,0:T(8,128)S(1)}, f32[2,544,128]{2,1,0:T(8,128)S(1)}, f32[8,560,128]{2,1,0:T(8,128)S(1)}, f32[2,560,128]{2,1,0:T(8,128)S(1)}, f32[...) custom-call(f32[296,256]{1,0:T(8,128)S(1)} %collective-permute-done., ...), custom_call_target="tpu_custom_call" | custom-call | tf_op jit(solution)/shard_map/step0/pallas_call | solution.py:440
  18.5 6.5 %collective-permute-done.1.refs_1_ = f32[184,256]{1,0:T(8,128)S(1)} collective-permute-done((f32[184,256]{1,0:T(8,128)S(1)}, f32[184,256]{1,0:T(8,128)S(1)}, u32[]{:S(2)}, u32[]{:S(2)}) %collective-permute-start.1) | collective-permute-done | bytes 188448 | tf_op jit(solution)/shard_map/ppermute | solution.py:37
  25.1 1.4 %step1.1 = (f32[2,560,128]{2,1,0:T(8,128)S(1)}, f32[2,544,128]{2,1,0:T(8,128)S(1)}, f32[8,560,128]{2,1,0:T(8,128)S(1)}, f32[2,560,128]{2,1,0:T(8,128)S(1)}, f32[...) custom-call(f32[296,256]{1,0:T(8,128)S(1)} %collective-permute-done., ...), custom_call_target="tpu_custom_call", output_to_operand_aliasing={{0}: (2, {}), {1}: (3, {}), {2}: (4, {}), {3}: (5, {}), {4}... | custom-call | tf_op jit(solution)/shard_map/step1/pallas_call | solution.py:440
  26.5 0.0 collective-permute-done.3.refs_3_
  26.5 0.0 collective-permute-done.2.refs_2_
  26.5 0.8 %step2.1 = (f32[2,560,128]{2,1,0:T(8,128)S(1)}, f32[2,544,128]{2,1,0:T(8,128)S(1)}, f32[8,560,128]{2,1,0:T(8,128)S(1)}, f32[2,560,128]{2,1,0:T(8,128)S(1)}, f32[...) custom-call(f32[296,256]{1,0:T(8,128)S(1)} %collective-permute-done., ...), custom_call_target="tpu_custom_call", output_to_operand_aliasing={{0}: (4, {}), {1}: (5, {}), {2}: (6, {}), {3}: (7, {}), {4}... | custom-call | tf_op jit(solution)/shard_map/step2/pallas_call | solution.py:440
  27.3 12.2 %all_to_all.11 = f32[32,1,128]{2,1,0:T(1,128)S(1)} all-to-all(f32[32,1,128]{2,1,0:T(1,128)S(1)} %bitcast.7), channel_id=1, replica_groups=mesh['circ'=4,'radax'=8] {'circ','radax'}, dimensions={0} | all-to-all | bytes 32768 | tf_op jit(solution)/shard_map/all_to_all | solution.py:456
  39.6 1.3 %finish.1 = (f32[512,256]{1,0:T(8,128)}, f32[512,256]{1,0:T(8,128)}) custom-call(f32[32,128]{1,0:T(8,128)S(1)} %bitcast.6, f32[2,560,128]{2,1,0:T(8,128)S(1)} %get-tuple-element.55.trace, f32[2,560,128]{2,1,0:T(8,128)S(1)} %get-tuple-element.56.image, f32[2,512,128]{2,1,0:T(8,128)S(1)} %get-tuple-element.57.second), custom_call_target="tpu_custom_call" | custom-call | tf_op jit(solution)/shard_map/finish/pallas_call | solution.py:458
Async XLA Ops:
  1.9 12.7 %collective-permute-start = (f32[296,256]{1,0:T(8,128)S(1)}, f32[296,256]{1,0:T(8,128)S(1)}, u32[]{:S(2)}, u32[]{:S(2)}) collective-permute-start(f32[296,256]{1,0:T(8,128)S(1)} %get-tuple-element.30), channel_id=1, source_target_pairs={{8,0},{16,8},{24,16},{0,24},{9,1},{17,9},{25,17},{1,25},{10,2},{18... | collective-permute-start | bytes 909320 | tf_op jit(solution)/shard_map/ppermute | solution.py:37
  7.0 18.1 %collective-permute-start.1 = (f32[184,256]{1,0:T(8,128)S(1)}, f32[184,256]{1,0:T(8,128)S(1)}, u32[]{:S(2)}, u32[]{:S(2)}) collective-permute-start(f32[184,256]{1,0:T(8,128)S(1)} %get-tuple-element.31), channel_id=1, source_target_pairs={{16,0},{24,8},{0,16},{8,24},{17,1},{25,9},{1,17},{9,25},{18,2},{26... | collective-permute-start | bytes 565256 | tf_op jit(solution)/shard_map/ppermute | solution.py:37
  7.0 19.5 %collective-permute-start.2 = (f32[96,256]{1,0:T(8,128)S(1)}, f32[96,256]{1,0:T(8,128)S(1)}, u32[]{:S(2)}, u32[]{:S(2)}) collective-permute-start(f32[96,256]{1,0:T(8,128)S(1)} %get-tuple-element.32), channel_id=1, source_target_pairs={{16,0},{24,8},{0,16},{8,24},{17,1},{25,9},{1,17},{9,25},{18,2},{26... | collective-permute-start | bytes 294920 | tf_op jit(solution)/shard_map/ppermute | solution.py:37
  9.9 16.6 %collective-permute-start.3 = (f32[24,256]{1,0:T(8,128)S(1)}, f32[24,256]{1,0:T(8,128)S(1)}, u32[]{:S(2)}, u32[]{:S(2)}) collective-permute-start(f32[24,256]{1,0:T(8,128)S(1)} %get-tuple-element.33), channel_id=1, source_target_pairs={{24,0},{0,8},{8,16},{16,24},{25,1},{1,9},{9,17},{17,25},{26,2},{2,... | collective-permute-start | bytes 73736 | tf_op jit(solution)/shard_map/ppermute | solution.py:37
  14.6 1.0 %copy-start = (f32[512,256]{1,0:T(8,128)S(1)}, f32[512,256]{1,0:T(8,128)}, u32[]{:S(2)}) copy-start(f32[512,256]{1,0:T(8,128)} %refs_1_.1) | copy-start | bytes 1572868
  15.6 1.0 %copy-start.1 = (f32[512,256]{1,0:T(8,128)S(1)}, f32[512,256]{1,0:T(8,128)}, u32[]{:S(2)}) copy-start(f32[512,256]{1,0:T(8,128)} %refs_2_.1) | copy-start | bytes 1572868

commit v3 on v2

--- a/solution.py
+++ b/solution.py
@@ -18,7 +18,8 @@
 HALO = 2 * SPAN
 TAPS = range(-REACH, REACH + 2)
 CHUNK = 64
-LATER = (1, 3)
+WRITES = 4
+LATER = (1, 4), (1, 2)
 VMEM = pl.BlockSpec(memory_space=pltpu.VMEM)
 PARAMS = pltpu.CompilerParams(vmem_limit_bytes=40 << 20)
 
@@ -177,6 +178,20 @@
                 out[row : row + count, :] = lines[...]
 
 
+def own_kernel(rows, b, cr, trace, coef, sems):
+    copies = []
+    for h in range(trace.shape[0]):
+        lanes = pl.ds(h * LANES, LANES)
+        copies.append(
+            pltpu.make_async_copy(b.at[:, lanes], trace.at[h, pl.ds(SUB + HALO, rows)], sems.at[2 * h])
+        )
+        copies.append(pltpu.make_async_copy(cr.at[:, lanes], coef.at[h, pl.ds(HALO, rows)], sems.at[2 * h + 1]))
+    for copy in copies:
+        copy.start()
+    for copy in copies:
+        copy.wait()
+
+
 STATE = ("trace", "coef", "taps", *STAGES, "sums")
 
 
@@ -184,11 +199,7 @@
     refs = list(refs)
     mail = refs[:count]
     refs = refs[count:]
-    if work["starts"]:
-        own, own_coef = refs[:2]
-        refs = refs[2:]
-    else:
-        refs = refs[len(STATE) :]
+    refs = refs[2 if work["starts"] else len(STATE) :]
     state = dict(zip(STATE, refs, strict=False))
     rest = refs[len(STATE) :]
     trace, coef, taps = state["trace"], state["coef"], state["taps"]
@@ -197,9 +208,6 @@
 
     for h in range(groups):
         lanes = slice(h * LANES, (h + 1) * LANES)
-        if work["starts"]:
-            trace[h, SUB + HALO : SUB + HALO + rows, :] = own[:, lanes]
-            coef[h, HALO : HALO + rows, :] = own_coef[:, lanes]
         for edge, m, row in opening:
             at = 0 if edge == "head" else HALO + rows
             trace[h, SUB + at : SUB + at + HALO, :] = mail[m][row : row + HALO, lanes]
@@ -294,9 +302,9 @@
     det = p_p * q_q - p_q * p_q
     y1 = (q_q * b_p - p_q * b_q) / det
     y2 = (p_p * b_q - p_q * b_p) / det
-    step = rows // 4
     copies = []
-    for i in range(rows // step):
+    for i in range(WRITES):
+        step = rows // WRITES
         at = i * step
         one = jnp.broadcast_to(y1, (step, LANES))
         two = jnp.broadcast_to(y2, (step, LANES))
@@ -326,7 +334,7 @@
     frame = rows + 2 * HALO
     held = frame + 2 * SUB
     whole, remainder = divmod(SLIDE, rows)
-    assert cols == W and rows % (4 * SUB) == 0 and remainder % SUB == 0
+    assert cols == W and rows % (WRITES * SUB) == 0 and remainder % SUB == 0
     assert HALO <= remainder <= rows - HALO
 
     assert rows % LANES == 0
@@ -335,7 +343,9 @@
     count_lines = rows // LANES
     spare = HALO - SPAN - REACH - 1
     assert count_lines <= spare
-    later = frame - up8((frame - cut) * LATER[0] // LATER[1])
+    later = cut + up8((frame - cut) * LATER[0][0] // LATER[0][1])
+    middle = cut - up8(cut * LATER[1][0] // LATER[1][1])
+    lines_above = frame - later - count_lines
     below, above = whole + 1, whole
 
     def stator_rows(first, last, low):
@@ -345,24 +355,25 @@
     edge = ("tail", [("trace", 0, HALO, 0), ("rotor", 0, SPAN, HALO)])
     start = ("head", [("trace", rows - HALO, HALO, 0), ("rotor", rows - SPAN, SPAN, HALO)])
     sent = [
-        (below, [stator_rows(0, cut, low_below), ("lines", 0, rows - cut, rows, 0)]),
-        (above, [stator_rows(cut, later, low_above), ("lines", None, 0, rows - cut + 2 * HALO, cut)]),
-        (above, [stator_rows(later, frame, low_above)]),
+        (above, [stator_rows(later, frame, low_above), ("lines", lines_above, 0, rows - cut + 2 * HALO, cut)]),
+        (below, [stator_rows(0, middle, low_below), ("lines", 0, rows - cut, rows, 0)]),
+        (below, [stator_rows(middle, cut, low_below)]),
+        (above, [stator_rows(cut, later, low_above)]),
         (1, [start]),
     ]
     if (below + 1) % count == 0:
-        sent[0][1].append(edge)
+        sent[1][1].append(edge)
     else:
         sent.append((-1, [edge]))
     messages, holds, heights = [], [], []
     for by, parts in sent:
         row, laid = 0, []
         for kind, what, *_ in parts:
-            if kind == "lines" and what is not None:
+            if kind == "lines":
                 laid.append((kind, what, None))
                 continue
             laid.append((kind, row, what))
-            row += up8(count_lines if kind == "lines" else sum(size for _, _, size, _ in what))
+            row += up8(sum(size for _, _, size, _ in what))
         messages.append((by, laid))
         holds.append([(kind, at, rest) for (kind, at, _), (_, _, *rest) in zip(laid, parts, strict=True)])
         heights.append(row)
@@ -406,8 +417,17 @@
     shapes["second"] = vmem(groups, rows, LANES)
     shapes["sums"] = vmem(5, SUB, LANES)
 
-    steps = [[0], [1], list(range(2, len(sent)))]
-    state, taken = None, []
+    steps = [[1, 2], [0], list(range(3, len(sent)))]
+    taken = []
+    state = pl.pallas_call(
+        functools.partial(own_kernel, rows),
+        out_shape=[shapes["trace"], shapes["coef"]],
+        in_specs=[pl.BlockSpec(memory_space=pltpu.HBM)] * 2,
+        out_specs=[VMEM] * 2,
+        scratch_shapes=[pltpu.SemaphoreType.DMA((2 * groups,))],
+        compiler_params=PARAMS,
+        name="own",
+    )(*(pltpu.with_memory_space_constraint(x, pltpu.HBM) for x in (right_side, coef_rotor)))
     for number, batch in enumerate(steps):
         opening, fills = [], []
         for m in batch:
@@ -423,7 +443,7 @@
                 else:
                     first, last = what
                     coefs.append((len(taken) - 1, at, first, last))
-                    known["coef"][max(first, spare) : last] = True
+                    known["coef"][max(first, spare) : min(last, frame - spare)] = True
         can = reachable(own, known["trace"], known["coef"], known["taps"])
         work = {"starts": number == 0}
         for name in STAGES:
@@ -442,13 +462,13 @@
                 step_kernel, rows, opening, closing, work, fills, list(coefs), len(taken)
             ),
             out_shape=out_shape,
-            in_specs=[VMEM] * (len(taken) + (2 if number == 0 else len(STATE))),
+            in_specs=[VMEM] * (len(taken) + len(state)),
             out_specs=[VMEM] * len(out_shape),
             scratch_shapes=[vmem(frame, LANES)] * 2,
-            input_output_aliases={} if number == 0 else {len(taken) + i: i for i in range(len(STATE))},
+            input_output_aliases={len(taken) + i: i for i in range(len(state))},
             compiler_params=PARAMS,
             name=f"step{number}",
-        )(*inputs, *([right_side, coef_rotor] if number == 0 else state))
+        )(*inputs, *state)
     *state, line = state
     assert done["second"][HALO : HALO + rows].all()
     state = dict(zip(STATE, state, strict=True))
@@ -463,7 +483,7 @@
         scratch_shapes=[
             vmem(rows, cols),
             vmem(rows, cols),
-            pltpu.SemaphoreType.DMA((4, 2)),
+            pltpu.SemaphoreType.DMA((WRITES, 2)),
         ],
         compiler_params=PARAMS,
         name="finish",

time: 41.1 us -> 40.3 us (0.981)
  local copies, waits for them, and re-layouts: 2.08 us -> 0 us
  Pallas kernels: 6.63 us -> 7.8 us
  starting transfers between devices: 8.03 us -> 9.17 us
  waiting for transfers between devices: 11.2 us -> 10.2 us
    unnamed x4 -> x0, local copies, waits for them, and re-layouts: 2.08 us -> none
    pallas_call x0 -> x1, Pallas kernels: none -> 1.22 us  [local(): pl.pallas_call(functools.partial(own_kernel, rows), out_shape=[shapes['tr...]
    ppermute x4 -> x5, starting transfers between devices: 8.03 us -> 9.17 us  [shifted(): return lax.ppermute(block, 'circ', route)]
    ppermute x4 -> x5, waiting for transfers between devices: 11.2 us -> 10.2 us  [shifted(): return lax.ppermute(block, 'circ', route)]
  transfers between devices with their start and end apart: 4 -> 5, of which waited for: 2 -> 2; matrix products, arithmetic and copies ran while one was open for 0% -> 0% of each run, Pallas kernels for 8% -> 11%
where the time goes in v3:
time: 40.3 us; the launch traced here: 40.1 us
  blocking collectives  12.3 us (31%)
  waiting for transfers between devices  10.2 us (25%)
  starting transfers between devices  9.17 us (23%)
  Pallas kernels  7.8 us (19%)
  between operations  0.69 us (2%)
    all_to_all x1, blocking collectives, local(): parts = lax.all_to_all(line, ('circ', 'radax'), 0, 0, tiled=True)  12.3 us
    ppermute x5, waiting for transfers between devices, shifted(): return lax.ppermute(block, 'circ', route)  10.2 us
    ppermute x5, starting transfers between devices, shifted(): return lax.ppermute(block, 'circ', route)  9.17 us
    pallas_call x3, Pallas kernels, local(): pl.pallas_call(functools.partial(step_kernel, rows, opening, closing, wor...  4 us
    pallas_call x1, Pallas kernels, local(): pl.pallas_call(functools.partial(finish_kernel, rows, groups), out_shape=...  1.31 us
    pallas_call x1, Pallas kernels, local(): pl.pallas_call(functools.partial(pack_kernel, rows, total_rows, messages)...  1.27 us
    pallas_call x1, Pallas kernels, local(): pl.pallas_call(functools.partial(own_kernel, rows), out_shape=[shapes['tr...  1.22 us
  transfers between devices with their start and end apart: 5, of which 2 were waited for; matrix products, arithmetic and copies ran while one was open for 0% of the time, Pallas kernels for 11%

profile of v3, /device:TPU:0, one launch (start us, length us, event | category | flops | bytes accessed | tf_op | source)
XLA Modules:
  0.0 40.1 jit_solution(3835758290304101260)
XLA Ops:
  0.6 1.3 %pack.1 = (f32[200,256]{1,0:T(8,128)S(1)}, f32[160,256]{1,0:T(8,128)S(1)}, f32[136,256]{1,0:T(8,128)S(1)}, f32[72,256]{1,0:T(8,128)S(1)}, f32[24,256]{1,0:T(8,128)S(1)}) custom-call(f32[512,256]{1,0:T(8,128)} %b.3, f32[512,256]{1,0:T(8,128)} %cr.3, f32[512,256]{1,0:T(8,128)} %cs.1, s32[4,128]{1,0:T(4,128)} %bitcast.8, f32[4,128]{1,0:T(4,128)} %bitcast.9), custom_call_target="tpu_custom_call" | custom-call | tf_op jit(solution)/shard_map/pack/pallas_call | solution.py:381
  1.9 4.1 %collective-permute-start.2 = (f32[200,256]{1,0:T(8,128)S(1)}, f32[200,256]{1,0:T(8,128)S(1)}, u32[]{:S(2)}, u32[]{:S(2)}) collective-permute-start(f32[200,256]{1,0:T(8,128)S(1)} %get-tuple-element.35), channel_id=1, source_target_pairs={{16,0},{24,8},{0,16},{8,24},{17,1},{25,9},{1,17},{9,25},{18,2},{26... | collective-permute-start | bytes 614408 | tf_op jit(solution)/shard_map/ppermute | solution.py:38
  6.0 1.3 %collective-permute-start = (f32[160,256]{1,0:T(8,128)S(1)}, f32[160,256]{1,0:T(8,128)S(1)}, u32[]{:S(2)}, u32[]{:S(2)}) collective-permute-start(f32[160,256]{1,0:T(8,128)S(1)} %get-tuple-element.33), channel_id=1, source_target_pairs={{8,0},{16,8},{24,16},{0,24},{9,1},{17,9},{25,17},{1,25},{10,2},{18... | collective-permute-start | bytes 491528 | tf_op jit(solution)/shard_map/ppermute | solution.py:38
  7.4 0.2 collective-permute-start.1
  7.5 2.0 %collective-permute-start.3 = (f32[72,256]{1,0:T(8,128)S(1)}, f32[72,256]{1,0:T(8,128)S(1)}, u32[]{:S(2)}, u32[]{:S(2)}) collective-permute-start(f32[72,256]{1,0:T(8,128)S(1)} %get-tuple-element.36), channel_id=1, source_target_pairs={{16,0},{24,8},{0,16},{8,24},{17,1},{25,9},{1,17},{9,25},{18,2},{26... | collective-permute-start | bytes 221192 | tf_op jit(solution)/shard_map/ppermute | solution.py:38
  9.5 1.6 %collective-permute-start.4 = (f32[24,256]{1,0:T(8,128)S(1)}, f32[24,256]{1,0:T(8,128)S(1)}, u32[]{:S(2)}, u32[]{:S(2)}) collective-permute-start(f32[24,256]{1,0:T(8,128)S(1)} %get-tuple-element.37), channel_id=1, source_target_pairs={{24,0},{0,8},{8,16},{16,24},{25,1},{1,9},{9,17},{17,25},{26,2},{2,... | collective-permute-start | bytes 73736 | tf_op jit(solution)/shard_map/ppermute | solution.py:38
  11.1 1.2 %own.1 = (f32[2,560,128]{2,1,0:T(8,128)S(1)}, f32[2,544,128]{2,1,0:T(8,128)S(1)}) custom-call(f32[512,256]{1,0:T(8,128)} %b.3, f32[512,256]{1,0:T(8,128)} %cr.3), custom_call_target="tpu_custom_call" | custom-call | tf_op jit(solution)/shard_map/own/pallas_call | solution.py:422
  12.3 5.6 %collective-permute-done.1.refs_1_ = f32[136,256]{1,0:T(8,128)S(1)} collective-permute-done((f32[136,256]{1,0:T(8,128)S(1)}, f32[136,256]{1,0:T(8,128)S(1)}, u32[]{:S(2)}, u32[]{:S(2)}) %collective-permute-start.1) | collective-permute-done | bytes 139296 | tf_op jit(solution)/shard_map/ppermute | solution.py:38
  17.9 0.0 collective-permute-done.refs_0_
  17.9 1.8 %step0.1 = (f32[2,560,128]{2,1,0:T(8,128)S(1)}, f32[2,544,128]{2,1,0:T(8,128)S(1)}, f32[8,560,128]{2,1,0:T(8,128)S(1)}, f32[2,560,128]{2,1,0:T(8,128)S(1)}, f32[...) custom-call(f32[160,256]{1,0:T(8,128)S(1)} %collective-permute-done., ...), custom_call_target="tpu_custom_call", output_to_operand_aliasing={{0}: (2, {}), {1}: (3, {})} | custom-call | tf_op jit(solution)/shard_map/step0/pallas_call | solution.py:460
  19.7 0.0 collective-permute-done.2.refs_2_
  19.7 1.4 %step1.1 = (f32[2,560,128]{2,1,0:T(8,128)S(1)}, f32[2,544,128]{2,1,0:T(8,128)S(1)}, f32[8,560,128]{2,1,0:T(8,128)S(1)}, f32[2,560,128]{2,1,0:T(8,128)S(1)}, f32[...) custom-call(f32[160,256]{1,0:T(8,128)S(1)} %collective-permute-done., ...), custom_call_target="tpu_custom_call", output_to_operand_aliasing={{0}: (3, {}), {1}: (4, {}), {2}: (5, {}), {3}: (6, {}), {4}... | custom-call | tf_op jit(solution)/shard_map/step1/pallas_call | solution.py:460
  21.2 0.0 collective-permute-done.4.refs_4_
  21.2 4.5 %collective-permute-done.3.refs_3_ = f32[72,256]{1,0:T(8,128)S(1)} collective-permute-done((f32[72,256]{1,0:T(8,128)S(1)}, f32[72,256]{1,0:T(8,128)S(1)}, u32[]{:S(2)}, u32[]{:S(2)}) %collective-permute-start.3) | collective-permute-done | bytes 73760 | tf_op jit(solution)/shard_map/ppermute | solution.py:38
  25.7 0.8 %step2.1 = (f32[2,560,128]{2,1,0:T(8,128)S(1)}, f32[2,544,128]{2,1,0:T(8,128)S(1)}, f32[8,560,128]{2,1,0:T(8,128)S(1)}, f32[2,560,128]{2,1,0:T(8,128)S(1)}, f32[...) custom-call(f32[160,256]{1,0:T(8,128)S(1)} %collective-permute-done., ...), custom_call_target="tpu_custom_call", output_to_operand_aliasing={{0}: (5, {}), {1}: (6, {}), {2}: (7, {}), {3}: (8, {}), {4}... | custom-call | tf_op jit(solution)/shard_map/step2/pallas_call | solution.py:460
  26.5 12.3 %all_to_all.11 = f32[32,1,128]{2,1,0:T(1,128)S(1)} all-to-all(f32[32,1,128]{2,1,0:T(1,128)S(1)} %bitcast.7), channel_id=1, replica_groups=mesh['circ'=4,'radax'=8] {'circ','radax'}, dimensions={0} | all-to-all | bytes 32768 | tf_op jit(solution)/shard_map/all_to_all | solution.py:476
  38.8 1.3 %finish.1 = (f32[512,256]{1,0:T(8,128)}, f32[512,256]{1,0:T(8,128)}) custom-call(f32[32,128]{1,0:T(8,128)S(1)} %bitcast.6, f32[2,560,128]{2,1,0:T(8,128)S(1)} %get-tuple-element.61.trace, f32[2,560,128]{2,1,0:T(8,128)S(1)} %get-tuple-element.62.image, f32[2,512,128]{2,1,0:T(8,128)S(1)} %get-tuple-element.63.second), custom_call_target="tpu_custom_call" | custom-call | tf_op jit(solution)/shard_map/finish/pallas_call | solution.py:478
Async XLA Ops:
  1.9 17.8 %collective-permute-start.2 = (f32[200,256]{1,0:T(8,128)S(1)}, f32[200,256]{1,0:T(8,128)S(1)}, u32[]{:S(2)}, u32[]{:S(2)}) collective-permute-start(f32[200,256]{1,0:T(8,128)S(1)} %get-tuple-element.35), channel_id=1, source_target_pairs={{16,0},{24,8},{0,16},{8,24},{17,1},{25,9},{1,17},{9,25},{18,2},{26... | collective-permute-start | bytes 614408 | tf_op jit(solution)/shard_map/ppermute | solution.py:38
  6.0 11.9 %collective-permute-start = (f32[160,256]{1,0:T(8,128)S(1)}, f32[160,256]{1,0:T(8,128)S(1)}, u32[]{:S(2)}, u32[]{:S(2)}) collective-permute-start(f32[160,256]{1,0:T(8,128)S(1)} %get-tuple-element.33), channel_id=1, source_target_pairs={{8,0},{16,8},{24,16},{0,24},{9,1},{17,9},{25,17},{1,25},{10,2},{18... | collective-permute-start | bytes 491528 | tf_op jit(solution)/shard_map/ppermute | solution.py:38
  7.4 10.6 %collective-permute-start.1 = (f32[136,256]{1,0:T(8,128)S(1)}, f32[136,256]{1,0:T(8,128)S(1)}, u32[]{:S(2)}, u32[]{:S(2)}) collective-permute-start(f32[136,256]{1,0:T(8,128)S(1)} %get-tuple-element.34), channel_id=1, source_target_pairs={{8,0},{16,8},{24,16},{0,24},{9,1},{17,9},{25,17},{1,25},{10,2},{18... | collective-permute-start | bytes 417800 | tf_op jit(solution)/shard_map/ppermute | solution.py:38
  7.5 18.2 %collective-permute-start.3 = (f32[72,256]{1,0:T(8,128)S(1)}, f32[72,256]{1,0:T(8,128)S(1)}, u32[]{:S(2)}, u32[]{:S(2)}) collective-permute-start(f32[72,256]{1,0:T(8,128)S(1)} %get-tuple-element.36), channel_id=1, source_target_pairs={{16,0},{24,8},{0,16},{8,24},{17,1},{25,9},{1,17},{9,25},{18,2},{26... | collective-permute-start | bytes 221192 | tf_op jit(solution)/shard_map/ppermute | solution.py:38
  9.5 11.7 %collective-permute-start.4 = (f32[24,256]{1,0:T(8,128)S(1)}, f32[24,256]{1,0:T(8,128)S(1)}, u32[]{:S(2)}, u32[]{:S(2)}) collective-permute-start(f32[24,256]{1,0:T(8,128)S(1)} %get-tuple-element.37), channel_id=1, source_target_pairs={{24,0},{0,8},{8,16},{16,24},{25,1},{1,9},{9,17},{17,25},{26,2},{2,... | collective-permute-start | bytes 73736 | tf_op jit(solution)/shard_map/ppermute | solution.py:38

commit v4 on v3

--- a/solution.py
+++ b/solution.py
@@ -136,6 +136,7 @@
 
 
 def pack_kernel(rows, total_rows, messages, b, cr, cs, mortar, weight, *refs):
+    refs = refs[len(refs) - len(messages) - 4 :]
     outs, (mortar_here, weight_here, lines, sems) = refs[: len(messages)], refs[len(messages) :]
     sources = {"trace": b, "rotor": cr, "stator": cs}
     small = [
@@ -377,32 +378,37 @@
         messages.append((by, laid))
         holds.append([(kind, at, rest) for (kind, at, _), (_, _, *rest) in zip(laid, parts, strict=True)])
         heights.append(row)
-    copies = sum(len(what) for _, laid in messages for kind, _, what in laid if kind != "lines")
-    packed = pl.pallas_call(
-        functools.partial(pack_kernel, rows, total_rows, messages),
-        out_shape=[vmem(height, cols) for height in heights],
-        in_specs=[pl.BlockSpec(memory_space=pltpu.HBM)] * 5,
-        out_specs=[VMEM] * len(messages),
-        scratch_shapes=[
-            pltpu.VMEM((count_lines, LANES), jnp.int32),
-            vmem(count_lines, LANES),
-            vmem(count_lines, cols),
-            pltpu.SemaphoreType.DMA((copies + 2,)),
-        ],
-        compiler_params=PARAMS,
-        name="pack",
-    )(
-        *(
-            pltpu.with_memory_space_constraint(x, pltpu.HBM)
-            for x in (
-                right_side,
-                coef_rotor,
-                coef_stator,
-                mortar_rows.reshape(count_lines, LANES),
-                mortar_weight.reshape(count_lines, LANES),
-            )
+    sources = [
+        pltpu.with_memory_space_constraint(x, pltpu.HBM)
+        for x in (
+            right_side,
+            coef_rotor,
+            coef_stator,
+            mortar_rows.reshape(count_lines, LANES),
+            mortar_weight.reshape(count_lines, LANES),
         )
-    )
+    ]
+
+    def pack(some, after):
+        laid = [messages[m] for m in some]
+        copies = sum(len(what) for _, parts in laid for kind, _, what in parts if kind != "lines")
+        return pl.pallas_call(
+            functools.partial(pack_kernel, rows, total_rows, laid),
+            out_shape=[vmem(heights[m], cols) for m in some],
+            in_specs=[pl.BlockSpec(memory_space=pltpu.HBM)] * 5 + [VMEM] * len(after),
+            out_specs=[VMEM] * len(some),
+            scratch_shapes=[
+                pltpu.VMEM((count_lines, LANES), jnp.int32),
+                vmem(count_lines, LANES),
+                vmem(count_lines, cols),
+                pltpu.SemaphoreType.DMA((copies + 2,)),
+            ],
+            compiler_params=PARAMS,
+            name="pack",
+        )(*sources, *after)
+
+    packed = pack([0], [])
+    packed += pack(range(1, len(messages)), packed)
     arrived = [shifted(block, by) for block, (by, _) in zip(packed, messages, strict=True)]
 
     own = np.zeros(frame, bool)
@@ -417,7 +423,7 @@
     shapes["second"] = vmem(groups, rows, LANES)
     shapes["sums"] = vmem(5, SUB, LANES)
 
-    steps = [[1, 2], [0], list(range(3, len(sent)))]
+    steps = [[1], [2], [0], list(range(3, len(sent)))]
     taken = []
     state = pl.pallas_call(
         functools.partial(own_kernel, rows),

time: 40.3 us -> 40 us (level)
  waiting for transfers between devices: 10.2 us -> 9.15 us
  Pallas kernels: 7.8 us -> 8.41 us
    ppermute x5, waiting for transfers between devices: 10.2 us -> 9.15 us  [shifted(): return lax.ppermute(block, 'circ', route)]
    pallas_call x1 -> x2, Pallas kernels: 1.27 us -> 2.16 us  [pack(): pl.pallas_call(functools.partial(pack_kernel, rows, total_rows, laid), ou...]
    pallas_call x3 -> x4, Pallas kernels: 4 us -> 3.73 us  [local(): pl.pallas_call(functools.partial(step_kernel, rows, opening, closing, wor...]
  transfers between devices with their start and end apart: 5 -> 5, of which waited for: 2 -> 3; matrix products, arithmetic and copies ran while one was open for 0% -> 0% of each run, Pallas kernels for 11% -> 13%
where the time goes in v4:
time: 40 us; the launch traced here: 39.8 us
  blocking collectives  12.3 us (31%)
  starting transfers between devices  9.22 us (23%)
  waiting for transfers between devices  9.15 us (23%)
  Pallas kernels  8.41 us (21%)
  between operations  0.7 us (2%)
    all_to_all x1, blocking collectives, local(): parts = lax.all_to_all(line, ('circ', 'radax'), 0, 0, tiled=True)  12.3 us
    ppermute x5, starting transfers between devices, shifted(): return lax.ppermute(block, 'circ', route)  9.22 us
    ppermute x5, waiting for transfers between devices, shifted(): return lax.ppermute(block, 'circ', route)  9.15 us
    pallas_call x4, Pallas kernels, local(): pl.pallas_call(functools.partial(step_kernel, rows, opening, closing, wor...  3.73 us
    pallas_call x2, Pallas kernels, pack(): pl.pallas_call(functools.partial(pack_kernel, rows, total_rows, laid), ou...  2.16 us
    pallas_call x1, Pallas kernels, local(): pl.pallas_call(functools.partial(finish_kernel, rows, groups), out_shape=...  1.31 us
    pallas_call x1, Pallas kernels, local(): pl.pallas_call(functools.partial(own_kernel, rows), out_shape=[shapes['tr...  1.22 us
  transfers between devices with their start and end apart: 5, of which 3 were waited for; matrix products, arithmetic and copies ran while one was open for 0% of the time, Pallas kernels for 13%

profile of v4, /device:TPU:0, one launch (start us, length us, event | category | flops | bytes accessed | tf_op | source)
XLA Modules:
  0.0 39.8 jit_solution(13066364343815676357)
XLA Ops:
  0.6 1.0 %pack.2.refs_0_ = f32[200,256]{1,0:T(8,128)S(1)} custom-call(f32[512,256]{1,0:T(8,128)} %b.5, f32[512,256]{1,0:T(8,128)} %cr.5, f32[512,256]{1,0:T(8,128)} %cs.3, s32[4,128]{1,0:T(4,128)} %bitcast.8, f32[4,128]{1,0:T(4,128)} %bitcast.10), custom_call_target="tpu_custom_call" | custom-call | tf_op jit(solution)/shard_map/pack/pallas_call | solution.py:395
  1.6 4.1 %collective-permute-start.2 = (f32[200,256]{1,0:T(8,128)S(1)}, f32[200,256]{1,0:T(8,128)S(1)}, u32[]{:S(2)}, u32[]{:S(2)}) collective-permute-start(f32[200,256]{1,0:T(8,128)S(1)} %pack.2.refs_0_), channel_id=1, source_target_pairs={{16,0},{24,8},{0,16},{8,24},{17,1},{25,9},{1,17},{9,25},{18,2},{26... | collective-permute-start | bytes 614408 | tf_op jit(solution)/shard_map/ppermute | solution.py:38
  5.7 1.2 %pack.3 = (f32[160,256]{1,0:T(8,128)S(1)}, f32[136,256]{1,0:T(8,128)S(1)}, f32[72,256]{1,0:T(8,128)S(1)}, f32[24,256]{1,0:T(8,128)S(1)}) custom-call(f32[512,256]{1,0:T(8,128)} %b.5, f32[512,256]{1,0:T(8,128)} %cr.5, f32[512,256]{1,0:T(8,128)} %cs.3, s32[4,128]{1,0:T(4,128)} %bitcast.9, f32[4,128]{1,0:T(4,128)} %bitcast.11, f32[200,256]{1,0:T(8,128)S(1)} %pack.2.refs_0_), custom_call_target="tpu_custom_call" | custom-call | tf_op jit(solution)/shard_map/pack/pallas_call | solution.py:395
  6.9 1.4 %collective-permute-start = (f32[160,256]{1,0:T(8,128)S(1)}, f32[160,256]{1,0:T(8,128)S(1)}, u32[]{:S(2)}, u32[]{:S(2)}) collective-permute-start(f32[160,256]{1,0:T(8,128)S(1)} %get-tuple-element.42), channel_id=1, source_target_pairs={{8,0},{16,8},{24,16},{0,24},{9,1},{17,9},{25,17},{1,25},{10,2},{18... | collective-permute-start | bytes 491528 | tf_op jit(solution)/shard_map/ppermute | solution.py:38
  8.3 0.1 collective-permute-start.1
  8.4 2.0 %collective-permute-start.3 = (f32[72,256]{1,0:T(8,128)S(1)}, f32[72,256]{1,0:T(8,128)S(1)}, u32[]{:S(2)}, u32[]{:S(2)}) collective-permute-start(f32[72,256]{1,0:T(8,128)S(1)} %get-tuple-element.44), channel_id=1, source_target_pairs={{16,0},{24,8},{0,16},{8,24},{17,1},{25,9},{1,17},{9,25},{18,2},{26... | collective-permute-start | bytes 221192 | tf_op jit(solution)/shard_map/ppermute | solution.py:38
  10.4 1.6 %collective-permute-start.4 = (f32[24,256]{1,0:T(8,128)S(1)}, f32[24,256]{1,0:T(8,128)S(1)}, u32[]{:S(2)}, u32[]{:S(2)}) collective-permute-start(f32[24,256]{1,0:T(8,128)S(1)} %get-tuple-element.45), channel_id=1, source_target_pairs={{24,0},{0,8},{8,16},{16,24},{25,1},{1,9},{9,17},{17,25},{26,2},{2,... | collective-permute-start | bytes 73736 | tf_op jit(solution)/shard_map/ppermute | solution.py:38
  12.0 1.2 %own.1 = (f32[2,560,128]{2,1,0:T(8,128)S(1)}, f32[2,544,128]{2,1,0:T(8,128)S(1)}) custom-call(f32[512,256]{1,0:T(8,128)} %b.5, f32[512,256]{1,0:T(8,128)} %cr.5), custom_call_target="tpu_custom_call" | custom-call | tf_op jit(solution)/shard_map/own/pallas_call | solution.py:428
  13.3 4.1 %collective-permute-done.refs_0_ = f32[160,256]{1,0:T(8,128)S(1)} collective-permute-done((f32[160,256]{1,0:T(8,128)S(1)}, f32[160,256]{1,0:T(8,128)S(1)}, u32[]{:S(2)}, u32[]{:S(2)}) %collective-permute-start) | collective-permute-done | bytes 163872 | tf_op jit(solution)/shard_map/ppermute | solution.py:38
  17.3 0.9 %step0.1 = (f32[2,560,128]{2,1,0:T(8,128)S(1)}, f32[2,544,128]{2,1,0:T(8,128)S(1)}, f32[8,560,128]{2,1,0:T(8,128)S(1)}, f32[2,560,128]{2,1,0:T(8,128)S(1)}, f32[...) custom-call(f32[160,256]{1,0:T(8,128)S(1)} %collective-permute-done., ...), custom_call_target="tpu_custom_call", output_to_operand_aliasing={{0}: (1, {}), {1}: (2, {})} | custom-call | tf_op jit(solution)/shard_map/step0/pallas_call | solution.py:466
  18.2 0.6 %collective-permute-done.1.refs_1_ = f32[136,256]{1,0:T(8,128)S(1)} collective-permute-done((f32[136,256]{1,0:T(8,128)S(1)}, f32[136,256]{1,0:T(8,128)S(1)}, u32[]{:S(2)}, u32[]{:S(2)}) %collective-permute-start.1) | collective-permute-done | bytes 139296 | tf_op jit(solution)/shard_map/ppermute | solution.py:38
  18.8 0.8 %step1.1 = (f32[2,560,128]{2,1,0:T(8,128)S(1)}, f32[2,544,128]{2,1,0:T(8,128)S(1)}, f32[8,560,128]{2,1,0:T(8,128)S(1)}, f32[2,560,128]{2,1,0:T(8,128)S(1)}, f32[...) custom-call(f32[160,256]{1,0:T(8,128)S(1)} %collective-permute-done., ...), custom_call_target="tpu_custom_call", output_to_operand_aliasing={{0}: (2, {}), {1}: (3, {}), {2}: (4, {}), {3}: (5, {}), {4}... | custom-call | tf_op jit(solution)/shard_map/step1/pallas_call | solution.py:466
  19.6 0.0 collective-permute-done.2.refs_2_
  19.6 1.3 %step2.1 = (f32[2,560,128]{2,1,0:T(8,128)S(1)}, f32[2,544,128]{2,1,0:T(8,128)S(1)}, f32[8,560,128]{2,1,0:T(8,128)S(1)}, f32[2,560,128]{2,1,0:T(8,128)S(1)}, f32[...) custom-call(f32[160,256]{1,0:T(8,128)S(1)} %collective-permute-done., ...), custom_call_target="tpu_custom_call", output_to_operand_aliasing={{0}: (3, {}), {1}: (4, {}), {2}: (5, {}), {3}: (6, {}), {4}... | custom-call | tf_op jit(solution)/shard_map/step2/pallas_call | solution.py:466
  21.0 0.0 collective-permute-done.4.refs_4_
  21.0 4.5 %collective-permute-done.3.refs_3_ = f32[72,256]{1,0:T(8,128)S(1)} collective-permute-done((f32[72,256]{1,0:T(8,128)S(1)}, f32[72,256]{1,0:T(8,128)S(1)}, u32[]{:S(2)}, u32[]{:S(2)}) %collective-permute-start.3) | collective-permute-done | bytes 73760 | tf_op jit(solution)/shard_map/ppermute | solution.py:38
  25.4 0.7 %step3.1 = (f32[2,560,128]{2,1,0:T(8,128)S(1)}, f32[2,544,128]{2,1,0:T(8,128)S(1)}, f32[8,560,128]{2,1,0:T(8,128)S(1)}, f32[2,560,128]{2,1,0:T(8,128)S(1)}, f32[...) custom-call(f32[160,256]{1,0:T(8,128)S(1)} %collective-permute-done., ...), custom_call_target="tpu_custom_call", output_to_operand_aliasing={{0}: (5, {}), {1}: (6, {}), {2}: (7, {}), {3}: (8, {}), {4}... | custom-call | tf_op jit(solution)/shard_map/step3/pallas_call | solution.py:466
  26.2 12.3 %all_to_all.11 = f32[32,1,128]{2,1,0:T(1,128)S(1)} all-to-all(f32[32,1,128]{2,1,0:T(1,128)S(1)} %bitcast.7), channel_id=1, replica_groups=mesh['circ'=4,'radax'=8] {'circ','radax'}, dimensions={0} | all-to-all | bytes 32768 | tf_op jit(solution)/shard_map/all_to_all | solution.py:482
  38.5 1.3 %finish.1 = (f32[512,256]{1,0:T(8,128)}, f32[512,256]{1,0:T(8,128)}) custom-call(f32[32,128]{1,0:T(8,128)S(1)} %bitcast.6, f32[2,560,128]{2,1,0:T(8,128)S(1)} %get-tuple-element.79.trace, f32[2,560,128]{2,1,0:T(8,128)S(1)} %get-tuple-element.80.image, f32[2,512,128]{2,1,0:T(8,128)S(1)} %get-tuple-element.81.second), custom_call_target="tpu_custom_call" | custom-call | tf_op jit(solution)/shard_map/finish/pallas_call | solution.py:484
Async XLA Ops:
  1.6 18.0 %collective-permute-start.2 = (f32[200,256]{1,0:T(8,128)S(1)}, f32[200,256]{1,0:T(8,128)S(1)}, u32[]{:S(2)}, u32[]{:S(2)}) collective-permute-start(f32[200,256]{1,0:T(8,128)S(1)} %pack.2.refs_0_), channel_id=1, source_target_pairs={{16,0},{24,8},{0,16},{8,24},{17,1},{25,9},{1,17},{9,25},{18,2},{26... | collective-permute-start | bytes 614408 | tf_op jit(solution)/shard_map/ppermute | solution.py:38
  6.9 10.4 %collective-permute-start = (f32[160,256]{1,0:T(8,128)S(1)}, f32[160,256]{1,0:T(8,128)S(1)}, u32[]{:S(2)}, u32[]{:S(2)}) collective-permute-start(f32[160,256]{1,0:T(8,128)S(1)} %get-tuple-element.42), channel_id=1, source_target_pairs={{8,0},{16,8},{24,16},{0,24},{9,1},{17,9},{25,17},{1,25},{10,2},{18... | collective-permute-start | bytes 491528 | tf_op jit(solution)/shard_map/ppermute | solution.py:38
  8.3 10.5 %collective-permute-start.1 = (f32[136,256]{1,0:T(8,128)S(1)}, f32[136,256]{1,0:T(8,128)S(1)}, u32[]{:S(2)}, u32[]{:S(2)}) collective-permute-start(f32[136,256]{1,0:T(8,128)S(1)} %get-tuple-element.43), channel_id=1, source_target_pairs={{8,0},{16,8},{24,16},{0,24},{9,1},{17,9},{25,17},{1,25},{10,2},{18... | collective-permute-start | bytes 417800 | tf_op jit(solution)/shard_map/ppermute | solution.py:38
  8.4 17.0 %collective-permute-start.3 = (f32[72,256]{1,0:T(8,128)S(1)}, f32[72,256]{1,0:T(8,128)S(1)}, u32[]{:S(2)}, u32[]{:S(2)}) collective-permute-start(f32[72,256]{1,0:T(8,128)S(1)} %get-tuple-element.44), channel_id=1, source_target_pairs={{16,0},{24,8},{0,16},{8,24},{17,1},{25,9},{1,17},{9,25},{18,2},{26... | collective-permute-start | bytes 221192 | tf_op jit(solution)/shard_map/ppermute | solution.py:38
  10.4 10.5 %collective-permute-start.4 = (f32[24,256]{1,0:T(8,128)S(1)}, f32[24,256]{1,0:T(8,128)S(1)}, u32[]{:S(2)}, u32[]{:S(2)}) collective-permute-start(f32[24,256]{1,0:T(8,128)S(1)} %get-tuple-element.45), channel_id=1, source_target_pairs={{24,0},{0,8},{8,16},{16,24},{25,1},{1,9},{9,17},{17,25},{26,2},{2,... | collective-permute-start | bytes 73736 | tf_op jit(solution)/shard_map/ppermute | solution.py:38

commit v5 on v4

--- a/solution.py
+++ b/solution.py
@@ -17,7 +17,7 @@
 SPAN = 2 * (REACH + 1)
 HALO = 2 * SPAN
 TAPS = range(-REACH, REACH + 2)
-CHUNK = 64
+CHUNK = 16
 WRITES = 4
 LATER = (1, 4), (1, 2)
 VMEM = pl.BlockSpec(memory_space=pltpu.VMEM)

time: 40 us -> 40 us (level)
  no operation moved by 1% of the time
where the time goes in v5:
time: 40 us; the launch traced here: 39.8 us
  blocking collectives  12.3 us (31%)
  waiting for transfers between devices  9.38 us (23%)
  starting transfers between devices  9.22 us (23%)
  Pallas kernels  8.17 us (20%)
  between operations  0.7 us (2%)
    all_to_all x1, blocking collectives, local(): parts = lax.all_to_all(line, ('circ', 'radax'), 0, 0, tiled=True)  12.3 us
    ppermute x5, waiting for transfers between devices, shifted(): return lax.ppermute(block, 'circ', route)  9.38 us
    ppermute x5, starting transfers between devices, shifted(): return lax.ppermute(block, 'circ', route)  9.22 us
    pallas_call x4, Pallas kernels, local(): pl.pallas_call(functools.partial(step_kernel, rows, opening, closing, wor...  3.48 us
    pallas_call x2, Pallas kernels, pack(): pl.pallas_call(functools.partial(pack_kernel, rows, total_rows, laid), ou...  2.16 us
    pallas_call x1, Pallas kernels, local(): pl.pallas_call(functools.partial(finish_kernel, rows, groups), out_shape=...  1.31 us
    pallas_call x1, Pallas kernels, local(): pl.pallas_call(functools.partial(own_kernel, rows), out_shape=[shapes['tr...  1.22 us
  transfers between devices with their start and end apart: 5, of which 3 were waited for; matrix products, arithmetic and copies ran while one was open for 0% of the time, Pallas kernels for 13%

profile of v5, /device:TPU:0, one launch (start us, length us, event | category | flops | bytes accessed | tf_op | source)
XLA Modules:
  0.0 39.8 jit_solution(1680868991816721321)
XLA Ops:
  0.6 1.0 %pack.2.refs_0_ = f32[200,256]{1,0:T(8,128)S(1)} custom-call(f32[512,256]{1,0:T(8,128)} %b.5, f32[512,256]{1,0:T(8,128)} %cr.5, f32[512,256]{1,0:T(8,128)} %cs.3, s32[4,128]{1,0:T(4,128)} %bitcast.8, f32[4,128]{1,0:T(4,128)} %bitcast.10), custom_call_target="tpu_custom_call" | custom-call | tf_op jit(solution)/shard_map/pack/pallas_call | solution.py:395
  1.6 4.1 %collective-permute-start.2 = (f32[200,256]{1,0:T(8,128)S(1)}, f32[200,256]{1,0:T(8,128)S(1)}, u32[]{:S(2)}, u32[]{:S(2)}) collective-permute-start(f32[200,256]{1,0:T(8,128)S(1)} %pack.2.refs_0_), channel_id=1, source_target_pairs={{16,0},{24,8},{0,16},{8,24},{17,1},{25,9},{1,17},{9,25},{18,2},{26... | collective-permute-start | bytes 614408 | tf_op jit(solution)/shard_map/ppermute | solution.py:38
  5.7 1.2 %pack.3 = (f32[160,256]{1,0:T(8,128)S(1)}, f32[136,256]{1,0:T(8,128)S(1)}, f32[72,256]{1,0:T(8,128)S(1)}, f32[24,256]{1,0:T(8,128)S(1)}) custom-call(f32[512,256]{1,0:T(8,128)} %b.5, f32[512,256]{1,0:T(8,128)} %cr.5, f32[512,256]{1,0:T(8,128)} %cs.3, s32[4,128]{1,0:T(4,128)} %bitcast.9, f32[4,128]{1,0:T(4,128)} %bitcast.11, f32[200,256]{1,0:T(8,128)S(1)} %pack.2.refs_0_), custom_call_target="tpu_custom_call" | custom-call | tf_op jit(solution)/shard_map/pack/pallas_call | solution.py:395
  6.9 1.4 %collective-permute-start = (f32[160,256]{1,0:T(8,128)S(1)}, f32[160,256]{1,0:T(8,128)S(1)}, u32[]{:S(2)}, u32[]{:S(2)}) collective-permute-start(f32[160,256]{1,0:T(8,128)S(1)} %get-tuple-element.42), channel_id=1, source_target_pairs={{8,0},{16,8},{24,16},{0,24},{9,1},{17,9},{25,17},{1,25},{10,2},{18... | collective-permute-start | bytes 491528 | tf_op jit(solution)/shard_map/ppermute | solution.py:38
  8.3 0.1 collective-permute-start.1
  8.4 2.0 %collective-permute-start.3 = (f32[72,256]{1,0:T(8,128)S(1)}, f32[72,256]{1,0:T(8,128)S(1)}, u32[]{:S(2)}, u32[]{:S(2)}) collective-permute-start(f32[72,256]{1,0:T(8,128)S(1)} %get-tuple-element.44), channel_id=1, source_target_pairs={{16,0},{24,8},{0,16},{8,24},{17,1},{25,9},{1,17},{9,25},{18,2},{26... | collective-permute-start | bytes 221192 | tf_op jit(solution)/shard_map/ppermute | solution.py:38
  10.4 1.6 %collective-permute-start.4 = (f32[24,256]{1,0:T(8,128)S(1)}, f32[24,256]{1,0:T(8,128)S(1)}, u32[]{:S(2)}, u32[]{:S(2)}) collective-permute-start(f32[24,256]{1,0:T(8,128)S(1)} %get-tuple-element.45), channel_id=1, source_target_pairs={{24,0},{0,8},{8,16},{16,24},{25,1},{1,9},{9,17},{17,25},{26,2},{2,... | collective-permute-start | bytes 73736 | tf_op jit(solution)/shard_map/ppermute | solution.py:38
  12.0 1.2 %own.1 = (f32[2,560,128]{2,1,0:T(8,128)S(1)}, f32[2,544,128]{2,1,0:T(8,128)S(1)}) custom-call(f32[512,256]{1,0:T(8,128)} %b.5, f32[512,256]{1,0:T(8,128)} %cr.5), custom_call_target="tpu_custom_call" | custom-call | tf_op jit(solution)/shard_map/own/pallas_call | solution.py:428
  13.3 4.1 %collective-permute-done.refs_0_ = f32[160,256]{1,0:T(8,128)S(1)} collective-permute-done((f32[160,256]{1,0:T(8,128)S(1)}, f32[160,256]{1,0:T(8,128)S(1)}, u32[]{:S(2)}, u32[]{:S(2)}) %collective-permute-start) | collective-permute-done | bytes 163872 | tf_op jit(solution)/shard_map/ppermute | solution.py:38
  17.3 0.8 %step0.1 = (f32[2,560,128]{2,1,0:T(8,128)S(1)}, f32[2,544,128]{2,1,0:T(8,128)S(1)}, f32[8,560,128]{2,1,0:T(8,128)S(1)}, f32[2,560,128]{2,1,0:T(8,128)S(1)}, f32[...) custom-call(f32[160,256]{1,0:T(8,128)S(1)} %collective-permute-done., ...), custom_call_target="tpu_custom_call", output_to_operand_aliasing={{0}: (1, {}), {1}: (2, {})} | custom-call | tf_op jit(solution)/shard_map/step0/pallas_call | solution.py:466
  18.1 0.7 %collective-permute-done.1.refs_1_ = f32[136,256]{1,0:T(8,128)S(1)} collective-permute-done((f32[136,256]{1,0:T(8,128)S(1)}, f32[136,256]{1,0:T(8,128)S(1)}, u32[]{:S(2)}, u32[]{:S(2)}) %collective-permute-start.1) | collective-permute-done | bytes 139296 | tf_op jit(solution)/shard_map/ppermute | solution.py:38
  18.8 0.7 %step1.1 = (f32[2,560,128]{2,1,0:T(8,128)S(1)}, f32[2,544,128]{2,1,0:T(8,128)S(1)}, f32[8,560,128]{2,1,0:T(8,128)S(1)}, f32[2,560,128]{2,1,0:T(8,128)S(1)}, f32[...) custom-call(f32[160,256]{1,0:T(8,128)S(1)} %collective-permute-done., ...), custom_call_target="tpu_custom_call", output_to_operand_aliasing={{0}: (2, {}), {1}: (3, {}), {2}: (4, {}), {3}: (5, {}), {4}... | custom-call | tf_op jit(solution)/shard_map/step1/pallas_call | solution.py:466
  19.5 0.0 collective-permute-done.2.refs_2_
  19.5 1.2 %step2.1 = (f32[2,560,128]{2,1,0:T(8,128)S(1)}, f32[2,544,128]{2,1,0:T(8,128)S(1)}, f32[8,560,128]{2,1,0:T(8,128)S(1)}, f32[2,560,128]{2,1,0:T(8,128)S(1)}, f32[...) custom-call(f32[160,256]{1,0:T(8,128)S(1)} %collective-permute-done., ...), custom_call_target="tpu_custom_call", output_to_operand_aliasing={{0}: (3, {}), {1}: (4, {}), {2}: (5, {}), {3}: (6, {}), {4}... | custom-call | tf_op jit(solution)/shard_map/step2/pallas_call | solution.py:466
  20.8 0.0 collective-permute-done.4.refs_4_
  20.8 4.6 %collective-permute-done.3.refs_3_ = f32[72,256]{1,0:T(8,128)S(1)} collective-permute-done((f32[72,256]{1,0:T(8,128)S(1)}, f32[72,256]{1,0:T(8,128)S(1)}, u32[]{:S(2)}, u32[]{:S(2)}) %collective-permute-start.3) | collective-permute-done | bytes 73760 | tf_op jit(solution)/shard_map/ppermute | solution.py:38
  25.4 0.7 %step3.1 = (f32[2,560,128]{2,1,0:T(8,128)S(1)}, f32[2,544,128]{2,1,0:T(8,128)S(1)}, f32[8,560,128]{2,1,0:T(8,128)S(1)}, f32[2,560,128]{2,1,0:T(8,128)S(1)}, f32[...) custom-call(f32[160,256]{1,0:T(8,128)S(1)} %collective-permute-done., ...), custom_call_target="tpu_custom_call", output_to_operand_aliasing={{0}: (5, {}), {1}: (6, {}), {2}: (7, {}), {3}: (8, {}), {4}... | custom-call | tf_op jit(solution)/shard_map/step3/pallas_call | solution.py:466
  26.2 12.3 %all_to_all.11 = f32[32,1,128]{2,1,0:T(1,128)S(1)} all-to-all(f32[32,1,128]{2,1,0:T(1,128)S(1)} %bitcast.7), channel_id=1, replica_groups=mesh['circ'=4,'radax'=8] {'circ','radax'}, dimensions={0} | all-to-all | bytes 32768 | tf_op jit(solution)/shard_map/all_to_all | solution.py:482
  38.5 1.3 %finish.1 = (f32[512,256]{1,0:T(8,128)}, f32[512,256]{1,0:T(8,128)}) custom-call(f32[32,128]{1,0:T(8,128)S(1)} %bitcast.6, f32[2,560,128]{2,1,0:T(8,128)S(1)} %get-tuple-element.79.trace, f32[2,560,128]{2,1,0:T(8,128)S(1)} %get-tuple-element.80.image, f32[2,512,128]{2,1,0:T(8,128)S(1)} %get-tuple-element.81.second), custom_call_target="tpu_custom_call" | custom-call | tf_op jit(solution)/shard_map/finish/pallas_call | solution.py:484
Async XLA Ops:
  1.6 17.9 %collective-permute-start.2 = (f32[200,256]{1,0:T(8,128)S(1)}, f32[200,256]{1,0:T(8,128)S(1)}, u32[]{:S(2)}, u32[]{:S(2)}) collective-permute-start(f32[200,256]{1,0:T(8,128)S(1)} %pack.2.refs_0_), channel_id=1, source_target_pairs={{16,0},{24,8},{0,16},{8,24},{17,1},{25,9},{1,17},{9,25},{18,2},{26... | collective-permute-start | bytes 614408 | tf_op jit(solution)/shard_map/ppermute | solution.py:38
  6.9 10.4 %collective-permute-start = (f32[160,256]{1,0:T(8,128)S(1)}, f32[160,256]{1,0:T(8,128)S(1)}, u32[]{:S(2)}, u32[]{:S(2)}) collective-permute-start(f32[160,256]{1,0:T(8,128)S(1)} %get-tuple-element.42), channel_id=1, source_target_pairs={{8,0},{16,8},{24,16},{0,24},{9,1},{17,9},{25,17},{1,25},{10,2},{18... | collective-permute-start | bytes 491528 | tf_op jit(solution)/shard_map/ppermute | solution.py:38
  8.3 10.5 %collective-permute-start.1 = (f32[136,256]{1,0:T(8,128)S(1)}, f32[136,256]{1,0:T(8,128)S(1)}, u32[]{:S(2)}, u32[]{:S(2)}) collective-permute-start(f32[136,256]{1,0:T(8,128)S(1)} %get-tuple-element.43), channel_id=1, source_target_pairs={{8,0},{16,8},{24,16},{0,24},{9,1},{17,9},{25,17},{1,25},{10,2},{18... | collective-permute-start | bytes 417800 | tf_op jit(solution)/shard_map/ppermute | solution.py:38
  8.4 17.0 %collective-permute-start.3 = (f32[72,256]{1,0:T(8,128)S(1)}, f32[72,256]{1,0:T(8,128)S(1)}, u32[]{:S(2)}, u32[]{:S(2)}) collective-permute-start(f32[72,256]{1,0:T(8,128)S(1)} %get-tuple-element.44), channel_id=1, source_target_pairs={{16,0},{24,8},{0,16},{8,24},{17,1},{25,9},{1,17},{9,25},{18,2},{26... | collective-permute-start | bytes 221192 | tf_op jit(solution)/shard_map/ppermute | solution.py:38
  10.4 10.3 %collective-permute-start.4 = (f32[24,256]{1,0:T(8,128)S(1)}, f32[24,256]{1,0:T(8,128)S(1)}, u32[]{:S(2)}, u32[]{:S(2)}) collective-permute-start(f32[24,256]{1,0:T(8,128)S(1)} %get-tuple-element.45), channel_id=1, source_target_pairs={{24,0},{0,8},{8,16},{16,24},{25,1},{1,9},{9,17},{17,25},{26,2},{2,... | collective-permute-start | bytes 73736 | tf_op jit(solution)/shard_map/ppermute | solution.py:38

commit v6 on v5

--- a/solution.py
+++ b/solution.py
@@ -78,6 +78,10 @@
     tiles = tiles.all(1) if whole else tiles.any(1)
     edges = np.flatnonzero(np.diff(np.concatenate([[0], tiles.astype(np.int8), [0]])))
     return [(int(a) * SUB, int(b) * SUB) for a, b in zip(edges[::2], edges[1::2], strict=True)]
+
+
+def clip(ranges, low, high):
+    return [(max(a, low), min(b, high)) for a, b in ranges if max(a, low) < min(b, high)]
 
 
 def for_chunks(ranges, body, carry=None):
@@ -179,9 +183,14 @@
                 out[row : row + count, :] = lines[...]
 
 
-def own_kernel(rows, b, cr, trace, coef, sems):
+def inner(rows):
+    return HALO + SUB, HALO + rows - SUB
+
+
+def own_kernel(rows, b, cr, trace, coef, base, sems):
+    groups = trace.shape[0]
     copies = []
-    for h in range(trace.shape[0]):
+    for h in range(groups):
         lanes = pl.ds(h * LANES, LANES)
         copies.append(
             pltpu.make_async_copy(b.at[:, lanes], trace.at[h, pl.ds(SUB + HALO, rows)], sems.at[2 * h])
@@ -192,15 +201,23 @@
     for copy in copies:
         copy.wait()
 
-
-STATE = ("trace", "coef", "taps", *STAGES, "sums")
+    def stencil(at, step, carry):
+        mid, total = around(trace, at, step)
+        for h in range(groups):
+            base[h, at : at + step, :] = coef[h, at : at + step, :] * mid[h] - 0.25 * total[h]
+        return carry
+
+    for_chunks([inner(rows)], stencil)
+
+
+STATE = ("trace", "coef", "base", "taps", *STAGES, "sums")
 
 
 def step_kernel(rows, opening, closing, work, fills, coefs, count, *refs):
     refs = list(refs)
     mail = refs[:count]
     refs = refs[count:]
-    refs = refs[2 if work["starts"] else len(STATE) :]
+    refs = refs[3 if work["starts"] else len(STATE) :]
     state = dict(zip(STATE, refs, strict=False))
     rest = refs[len(STATE) :]
     trace, coef, taps = state["trace"], state["coef"], state["taps"]
@@ -252,7 +269,7 @@
                     target[h, at + SUB : at + SUB + step, :] = scale * mid[h] - 0.25 * total[h]
                 return carry
 
-            for_chunks([(max(a, first), min(b, end)) for a, b in ranges if max(a, first) < min(b, end)], body)
+            for_chunks(clip(ranges, first, end), body)
 
     def apply(source, response, at, step):
         mid, total = around(source, at, step)
@@ -261,6 +278,12 @@
 
     def first_image(at, step, carry):
         for h, value in enumerate(apply(trace, state["resp"], at, step)[1]):
+            state["image"][h, at + SUB : at + SUB + step, :] = value
+        return carry
+
+    def inner_image(at, step, carry):
+        acc = [state["base"][h, at : at + step, :] for h in range(groups)]
+        for h, value in enumerate(give_back(taps, state["resp"], at, step, acc)):
             state["image"][h, at + SUB : at + SUB + step, :] = value
         return carry
 
@@ -277,7 +300,9 @@
 
     for_chunks(work["proj"], plain_project(trace, state["proj"]))
     respond(state["proj"], state["resp"], work["resp"])
-    for_chunks(work["image"], first_image)
+    low, high = inner(rows)
+    for_chunks(clip(work["image"], 0, low) + clip(work["image"], high, frame), first_image)
+    for_chunks(clip(work["image"], low, high), inner_image)
     for_chunks(work["proj_two"], plain_project(state["image"], state["proj_two"]))
     respond(state["proj_two"], state["resp_two"], work["resp_two"])
     if work["starts"]:
@@ -289,12 +314,11 @@
         lane = lax.broadcasted_iota(jnp.int32, (SUB, LANES), 1)
         line = jnp.zeros((SUB, LANES), jnp.float32)
         for j, total in enumerate(totals):
-            line = jnp.where(lane == j, jnp.sum(total), line)
-        rest[0][...] = jnp.broadcast_to(line[0:1], rest[0].shape)
+            line = jnp.where(lane == j, jnp.sum(total, axis=1, keepdims=True), line)
+        rest[0][...] = jnp.broadcast_to(jnp.sum(line, axis=0, keepdims=True), rest[0].shape)
     else:
         for j, total in enumerate(totals):
             state["sums"][j] = total
-    del frame
 
 
 def finish_kernel(rows, groups, parts, trace, image, second, solution_out, residual_out, sol, res, sems):
@@ -418,7 +442,7 @@
     want = needed(own)
     coefs = []
     shapes = {name: vmem(groups, held, LANES) for name in STATE}
-    shapes["coef"] = vmem(groups, frame, LANES)
+    shapes["coef"] = shapes["base"] = vmem(groups, frame, LANES)
     shapes["taps"] = vmem(len(TAPS), held, LANES)
     shapes["second"] = vmem(groups, rows, LANES)
     shapes["sums"] = vmem(5, SUB, LANES)
@@ -427,9 +451,9 @@
     taken = []
     state = pl.pallas_call(
         functools.partial(own_kernel, rows),
-        out_shape=[shapes["trace"], shapes["coef"]],
+        out_shape=[shapes["trace"], shapes["coef"], shapes["base"]],
         in_specs=[pl.BlockSpec(memory_space=pltpu.HBM)] * 2,
-        out_specs=[VMEM] * 2,
+        out_specs=[VMEM] * 3,
         scratch_shapes=[pltpu.SemaphoreType.DMA((2 * groups,))],
         compiler_params=PARAMS,
         name="own",

time: 40 us -> 39.9 us (level)
  no operation moved by 1% of the time
where the time goes in v6:
time: 39.9 us; the launch traced here: 39.7 us
  blocking collectives  12.3 us (31%)
  waiting for transfers between devices  9.24 us (23%)
  starting transfers between devices  9.22 us (23%)
  Pallas kernels  8.22 us (21%)
  between operations  0.69 us (2%)
    all_to_all x1, blocking collectives, local(): parts = lax.all_to_all(line, ('circ', 'radax'), 0, 0, tiled=True)  12.3 us
    ppermute x5, waiting for transfers between devices, shifted(): return lax.ppermute(block, 'circ', route)  9.24 us
    ppermute x5, starting transfers between devices, shifted(): return lax.ppermute(block, 'circ', route)  9.22 us
    pallas_call x4, Pallas kernels, local(): pl.pallas_call(functools.partial(step_kernel, rows, opening, closing, wor...  3.21 us
    pallas_call x2, Pallas kernels, pack(): pl.pallas_call(functools.partial(pack_kernel, rows, total_rows, laid), ou...  2.16 us
    pallas_call x1, Pallas kernels, local(): pl.pallas_call(functools.partial(own_kernel, rows), out_shape=[shapes['tr...  1.55 us
    pallas_call x1, Pallas kernels, local(): pl.pallas_call(functools.partial(finish_kernel, rows, groups), out_shape=...  1.31 us
  transfers between devices with their start and end apart: 5, of which 3 were waited for; matrix products, arithmetic and copies ran while one was open for 0% of the time, Pallas kernels for 13%

profile of v6, /device:TPU:0, one launch (start us, length us, event | category | flops | bytes accessed | tf_op | source)
XLA Modules:
  0.0 39.7 jit_solution(5064142466007685093)
XLA Ops:
  0.6 1.0 %pack.2.refs_0_ = f32[200,256]{1,0:T(8,128)S(1)} custom-call(f32[512,256]{1,0:T(8,128)} %b.5, f32[512,256]{1,0:T(8,128)} %cr.5, f32[512,256]{1,0:T(8,128)} %cs.3, s32[4,128]{1,0:T(4,128)} %bitcast.8, f32[4,128]{1,0:T(4,128)} %bitcast.10), custom_call_target="tpu_custom_call" | custom-call | tf_op jit(solution)/shard_map/pack/pallas_call | solution.py:419
  1.6 4.1 %collective-permute-start.2 = (f32[200,256]{1,0:T(8,128)S(1)}, f32[200,256]{1,0:T(8,128)S(1)}, u32[]{:S(2)}, u32[]{:S(2)}) collective-permute-start(f32[200,256]{1,0:T(8,128)S(1)} %pack.2.refs_0_), channel_id=1, source_target_pairs={{16,0},{24,8},{0,16},{8,24},{17,1},{25,9},{1,17},{9,25},{18,2},{26... | collective-permute-start | bytes 614408 | tf_op jit(solution)/shard_map/ppermute | solution.py:38
  5.7 1.2 %pack.3 = (f32[160,256]{1,0:T(8,128)S(1)}, f32[136,256]{1,0:T(8,128)S(1)}, f32[72,256]{1,0:T(8,128)S(1)}, f32[24,256]{1,0:T(8,128)S(1)}) custom-call(f32[512,256]{1,0:T(8,128)} %b.5, f32[512,256]{1,0:T(8,128)} %cr.5, f32[512,256]{1,0:T(8,128)} %cs.3, s32[4,128]{1,0:T(4,128)} %bitcast.9, f32[4,128]{1,0:T(4,128)} %bitcast.11, f32[200,256]{1,0:T(8,128)S(1)} %pack.2.refs_0_), custom_call_target="tpu_custom_call" | custom-call | tf_op jit(solution)/shard_map/pack/pallas_call | solution.py:419
  6.9 1.4 %collective-permute-start = (f32[160,256]{1,0:T(8,128)S(1)}, f32[160,256]{1,0:T(8,128)S(1)}, u32[]{:S(2)}, u32[]{:S(2)}) collective-permute-start(f32[160,256]{1,0:T(8,128)S(1)} %get-tuple-element.46), channel_id=1, source_target_pairs={{8,0},{16,8},{24,16},{0,24},{9,1},{17,9},{25,17},{1,25},{10,2},{18... | collective-permute-start | bytes 491528 | tf_op jit(solution)/shard_map/ppermute | solution.py:38
  8.3 0.1 collective-permute-start.1
  8.4 2.0 %collective-permute-start.3 = (f32[72,256]{1,0:T(8,128)S(1)}, f32[72,256]{1,0:T(8,128)S(1)}, u32[]{:S(2)}, u32[]{:S(2)}) collective-permute-start(f32[72,256]{1,0:T(8,128)S(1)} %get-tuple-element.48), channel_id=1, source_target_pairs={{16,0},{24,8},{0,16},{8,24},{17,1},{25,9},{1,17},{9,25},{18,2},{26... | collective-permute-start | bytes 221192 | tf_op jit(solution)/shard_map/ppermute | solution.py:38
  10.4 1.6 %collective-permute-start.4 = (f32[24,256]{1,0:T(8,128)S(1)}, f32[24,256]{1,0:T(8,128)S(1)}, u32[]{:S(2)}, u32[]{:S(2)}) collective-permute-start(f32[24,256]{1,0:T(8,128)S(1)} %get-tuple-element.49), channel_id=1, source_target_pairs={{24,0},{0,8},{8,16},{16,24},{25,1},{1,9},{9,17},{17,25},{26,2},{2,... | collective-permute-start | bytes 73736 | tf_op jit(solution)/shard_map/ppermute | solution.py:38
  12.0 1.6 %own.1 = (f32[2,560,128]{2,1,0:T(8,128)S(1)}, f32[2,544,128]{2,1,0:T(8,128)S(1)}, f32[2,544,128]{2,1,0:T(8,128)S(1)}) custom-call(f32[512,256]{1,0:T(8,128)} %b.5, f32[512,256]{1,0:T(8,128)} %cr.5), custom_call_target="tpu_custom_call" | custom-call | tf_op jit(solution)/shard_map/own/pallas_call | solution.py:452
  13.6 3.7 %collective-permute-done.refs_0_ = f32[160,256]{1,0:T(8,128)S(1)} collective-permute-done((f32[160,256]{1,0:T(8,128)S(1)}, f32[160,256]{1,0:T(8,128)S(1)}, u32[]{:S(2)}, u32[]{:S(2)}) %collective-permute-start) | collective-permute-done | bytes 163872 | tf_op jit(solution)/shard_map/ppermute | solution.py:38
  17.3 0.8 %step0.1 = (f32[2,560,128]{2,1,0:T(8,128)S(1)}, f32[2,544,128]{2,1,0:T(8,128)S(1)}, f32[2,544,128]{2,1,0:T(8,128)S(1)}, f32[8,560,128]{2,1,0:T(8,128)S(1)}, f32[...) custom-call(f32[160,256]{1,0:T(8,128)S(1)} %collective-permute-done., ...), custom_call_target="tpu_custom_call", output_to_operand_aliasing={{0}: (1, {}), {1}: (2, {}), {2}: (3, {})} | custom-call | tf_op jit(solution)/shard_map/step0/pallas_call | solution.py:490
  18.1 0.7 %collective-permute-done.1.refs_1_ = f32[136,256]{1,0:T(8,128)S(1)} collective-permute-done((f32[136,256]{1,0:T(8,128)S(1)}, f32[136,256]{1,0:T(8,128)S(1)}, u32[]{:S(2)}, u32[]{:S(2)}) %collective-permute-start.1) | collective-permute-done | bytes 139296 | tf_op jit(solution)/shard_map/ppermute | solution.py:38
  18.8 0.6 %step1.1 = (f32[2,560,128]{2,1,0:T(8,128)S(1)}, f32[2,544,128]{2,1,0:T(8,128)S(1)}, f32[2,544,128]{2,1,0:T(8,128)S(1)}, f32[8,560,128]{2,1,0:T(8,128)S(1)}, f32[...) custom-call(f32[160,256]{1,0:T(8,128)S(1)} %collective-permute-done., ...), custom_call_target="tpu_custom_call", output_to_operand_aliasing={{0}: (2, {}), {1}: (3, {}), {2}: (4, {}), {3}: (5, {}), {4}... | custom-call | tf_op jit(solution)/shard_map/step1/pallas_call | solution.py:490
  19.5 0.0 collective-permute-done.2.refs_2_
  19.5 1.2 %step2.1 = (f32[2,560,128]{2,1,0:T(8,128)S(1)}, f32[2,544,128]{2,1,0:T(8,128)S(1)}, f32[2,544,128]{2,1,0:T(8,128)S(1)}, f32[8,560,128]{2,1,0:T(8,128)S(1)}, f32[...) custom-call(f32[160,256]{1,0:T(8,128)S(1)} %collective-permute-done., ...), custom_call_target="tpu_custom_call", output_to_operand_aliasing={{0}: (3, {}), {1}: (4, {}), {2}: (5, {}), {3}: (6, {}), {4}... | custom-call | tf_op jit(solution)/shard_map/step2/pallas_call | solution.py:490
  20.6 0.0 collective-permute-done.4.refs_4_
  20.7 4.8 %collective-permute-done.3.refs_3_ = f32[72,256]{1,0:T(8,128)S(1)} collective-permute-done((f32[72,256]{1,0:T(8,128)S(1)}, f32[72,256]{1,0:T(8,128)S(1)}, u32[]{:S(2)}, u32[]{:S(2)}) %collective-permute-start.3) | collective-permute-done | bytes 73760 | tf_op jit(solution)/shard_map/ppermute | solution.py:38
  25.4 0.6 %step3.1 = (f32[2,560,128]{2,1,0:T(8,128)S(1)}, f32[2,544,128]{2,1,0:T(8,128)S(1)}, f32[2,544,128]{2,1,0:T(8,128)S(1)}, f32[8,560,128]{2,1,0:T(8,128)S(1)}, f32[...) custom-call(f32[160,256]{1,0:T(8,128)S(1)} %collective-permute-done., ...), custom_call_target="tpu_custom_call", output_to_operand_aliasing={{0}: (5, {}), {1}: (6, {}), {2}: (7, {}), {3}: (8, {}), {4}... | custom-call | tf_op jit(solution)/shard_map/step3/pallas_call | solution.py:490
  26.1 12.3 %all_to_all.11 = f32[32,1,128]{2,1,0:T(1,128)S(1)} all-to-all(f32[32,1,128]{2,1,0:T(1,128)S(1)} %bitcast.7), channel_id=1, replica_groups=mesh['circ'=4,'radax'=8] {'circ','radax'}, dimensions={0} | all-to-all | bytes 32768 | tf_op jit(solution)/shard_map/all_to_all | solution.py:506
  38.4 1.3 %finish.1 = (f32[512,256]{1,0:T(8,128)}, f32[512,256]{1,0:T(8,128)}) custom-call(f32[32,128]{1,0:T(8,128)S(1)} %bitcast.6, f32[2,560,128]{2,1,0:T(8,128)S(1)} %get-tuple-element.87.trace, f32[2,560,128]{2,1,0:T(8,128)S(1)} %get-tuple-element.88.image, f32[2,512,128]{2,1,0:T(8,128)S(1)} %get-tuple-element.89.second), custom_call_target="tpu_custom_call" | custom-call | tf_op jit(solution)/shard_map/finish/pallas_call | solution.py:508
Async XLA Ops:
  1.6 17.8 %collective-permute-start.2 = (f32[200,256]{1,0:T(8,128)S(1)}, f32[200,256]{1,0:T(8,128)S(1)}, u32[]{:S(2)}, u32[]{:S(2)}) collective-permute-start(f32[200,256]{1,0:T(8,128)S(1)} %pack.2.refs_0_), channel_id=1, source_target_pairs={{16,0},{24,8},{0,16},{8,24},{17,1},{25,9},{1,17},{9,25},{18,2},{26... | collective-permute-start | bytes 614408 | tf_op jit(solution)/shard_map/ppermute | solution.py:38
  6.9 10.4 %collective-permute-start = (f32[160,256]{1,0:T(8,128)S(1)}, f32[160,256]{1,0:T(8,128)S(1)}, u32[]{:S(2)}, u32[]{:S(2)}) collective-permute-start(f32[160,256]{1,0:T(8,128)S(1)} %get-tuple-element.46), channel_id=1, source_target_pairs={{8,0},{16,8},{24,16},{0,24},{9,1},{17,9},{25,17},{1,25},{10,2},{18... | collective-permute-start | bytes 491528 | tf_op jit(solution)/shard_map/ppermute | solution.py:38
  8.3 10.5 %collective-permute-start.1 = (f32[136,256]{1,0:T(8,128)S(1)}, f32[136,256]{1,0:T(8,128)S(1)}, u32[]{:S(2)}, u32[]{:S(2)}) collective-permute-start(f32[136,256]{1,0:T(8,128)S(1)} %get-tuple-element.47), channel_id=1, source_target_pairs={{8,0},{16,8},{24,16},{0,24},{9,1},{17,9},{25,17},{1,25},{10,2},{18... | collective-permute-start | bytes 417800 | tf_op jit(solution)/shard_map/ppermute | solution.py:38
  8.4 17.0 %collective-permute-start.3 = (f32[72,256]{1,0:T(8,128)S(1)}, f32[72,256]{1,0:T(8,128)S(1)}, u32[]{:S(2)}, u32[]{:S(2)}) collective-permute-start(f32[72,256]{1,0:T(8,128)S(1)} %get-tuple-element.48), channel_id=1, source_target_pairs={{16,0},{24,8},{0,16},{8,24},{17,1},{25,9},{1,17},{9,25},{18,2},{26... | collective-permute-start | bytes 221192 | tf_op jit(solution)/shard_map/ppermute | solution.py:38
  10.4 10.2 %collective-permute-start.4 = (f32[24,256]{1,0:T(8,128)S(1)}, f32[24,256]{1,0:T(8,128)S(1)}, u32[]{:S(2)}, u32[]{:S(2)}) collective-permute-start(f32[24,256]{1,0:T(8,128)S(1)} %get-tuple-element.49), channel_id=1, source_target_pairs={{24,0},{0,8},{8,16},{16,24},{25,1},{1,9},{9,17},{17,25},{26,2},{2,... | collective-permute-start | bytes 73736 | tf_op jit(solution)/shard_map/ppermute | solution.py:38

commit v7 on v6

--- a/solution.py
+++ b/solution.py
@@ -19,7 +19,7 @@
 TAPS = range(-REACH, REACH + 2)
 CHUNK = 16
 WRITES = 4
-LATER = (1, 4), (1, 2)
+LATER = (1, 5), (1, 2)
 VMEM = pl.BlockSpec(memory_space=pltpu.VMEM)
 PARAMS = pltpu.CompilerParams(vmem_limit_bytes=40 << 20)
 

time: 39.9 us -> 39.9 us (level)
  no operation moved by 1% of the time
where the time goes in v7:
time: 39.9 us; the launch traced here: 39.7 us
  blocking collectives  12.4 us (31%)
  starting transfers between devices  9.22 us (23%)
  waiting for transfers between devices  9.19 us (23%)
  Pallas kernels  8.19 us (21%)
  between operations  0.69 us (2%)
    all_to_all x1, blocking collectives, local(): parts = lax.all_to_all(line, ('circ', 'radax'), 0, 0, tiled=True)  12.4 us
    ppermute x5, starting transfers between devices, shifted(): return lax.ppermute(block, 'circ', route)  9.22 us
    ppermute x5, waiting for transfers between devices, shifted(): return lax.ppermute(block, 'circ', route)  9.19 us
    pallas_call x4, Pallas kernels, local(): pl.pallas_call(functools.partial(step_kernel, rows, opening, closing, wor...  3.21 us
    pallas_call x2, Pallas kernels, pack(): pl.pallas_call(functools.partial(pack_kernel, rows, total_rows, laid), ou...  2.12 us
    pallas_call x1, Pallas kernels, local(): pl.pallas_call(functools.partial(own_kernel, rows), out_shape=[shapes['tr...  1.55 us
    pallas_call x1, Pallas kernels, local(): pl.pallas_call(functools.partial(finish_kernel, rows, groups), out_shape=...  1.31 us
  transfers between devices with their start and end apart: 5, of which 3 were waited for; matrix products, arithmetic and copies ran while one was open for 0% of the time, Pallas kernels for 13%

profile of v7, /device:TPU:0, one launch (start us, length us, event | category | flops | bytes accessed | tf_op | source)
XLA Modules:
  0.0 39.7 jit_solution(5826802653409067875)
XLA Ops:
  0.6 1.0 %pack.2.refs_0_ = f32[216,256]{1,0:T(8,128)S(1)} custom-call(f32[512,256]{1,0:T(8,128)} %b.5, f32[512,256]{1,0:T(8,128)} %cr.5, f32[512,256]{1,0:T(8,128)} %cs.3, s32[4,128]{1,0:T(4,128)} %bitcast.8, f32[4,128]{1,0:T(4,128)} %bitcast.10), custom_call_target="tpu_custom_call" | custom-call | tf_op jit(solution)/shard_map/pack/pallas_call | solution.py:419
  1.6 4.1 %collective-permute-start.2 = (f32[216,256]{1,0:T(8,128)S(1)}, f32[216,256]{1,0:T(8,128)S(1)}, u32[]{:S(2)}, u32[]{:S(2)}) collective-permute-start(f32[216,256]{1,0:T(8,128)S(1)} %pack.2.refs_0_), channel_id=1, source_target_pairs={{16,0},{24,8},{0,16},{8,24},{17,1},{25,9},{1,17},{9,25},{18,2},{26... | collective-permute-start | bytes 663560 | tf_op jit(solution)/shard_map/ppermute | solution.py:38
  5.7 1.1 %pack.3 = (f32[160,256]{1,0:T(8,128)S(1)}, f32[136,256]{1,0:T(8,128)S(1)}, f32[56,256]{1,0:T(8,128)S(1)}, f32[24,256]{1,0:T(8,128)S(1)}) custom-call(f32[512,256]{1,0:T(8,128)} %b.5, f32[512,256]{1,0:T(8,128)} %cr.5, f32[512,256]{1,0:T(8,128)} %cs.3, s32[4,128]{1,0:T(4,128)} %bitcast.9, f32[4,128]{1,0:T(4,128)} %bitcast.11, f32[216,256]{1,0:T(8,128)S(1)} %pack.2.refs_0_), custom_call_target="tpu_custom_call" | custom-call | tf_op jit(solution)/shard_map/pack/pallas_call | solution.py:419
  6.9 1.4 %collective-permute-start = (f32[160,256]{1,0:T(8,128)S(1)}, f32[160,256]{1,0:T(8,128)S(1)}, u32[]{:S(2)}, u32[]{:S(2)}) collective-permute-start(f32[160,256]{1,0:T(8,128)S(1)} %get-tuple-element.46), channel_id=1, source_target_pairs={{8,0},{16,8},{24,16},{0,24},{9,1},{17,9},{25,17},{1,25},{10,2},{18... | collective-permute-start | bytes 491528 | tf_op jit(solution)/shard_map/ppermute | solution.py:38
  8.3 0.1 collective-permute-start.1
  8.4 2.0 %collective-permute-start.3 = (f32[56,256]{1,0:T(8,128)S(1)}, f32[56,256]{1,0:T(8,128)S(1)}, u32[]{:S(2)}, u32[]{:S(2)}) collective-permute-start(f32[56,256]{1,0:T(8,128)S(1)} %get-tuple-element.48), channel_id=1, source_target_pairs={{16,0},{24,8},{0,16},{8,24},{17,1},{25,9},{1,17},{9,25},{18,2},{26... | collective-permute-start | bytes 172040 | tf_op jit(solution)/shard_map/ppermute | solution.py:38
  10.4 1.6 %collective-permute-start.4 = (f32[24,256]{1,0:T(8,128)S(1)}, f32[24,256]{1,0:T(8,128)S(1)}, u32[]{:S(2)}, u32[]{:S(2)}) collective-permute-start(f32[24,256]{1,0:T(8,128)S(1)} %get-tuple-element.49), channel_id=1, source_target_pairs={{24,0},{0,8},{8,16},{16,24},{25,1},{1,9},{9,17},{17,25},{26,2},{2,... | collective-permute-start | bytes 73736 | tf_op jit(solution)/shard_map/ppermute | solution.py:38
  12.0 1.6 %own.1 = (f32[2,560,128]{2,1,0:T(8,128)S(1)}, f32[2,544,128]{2,1,0:T(8,128)S(1)}, f32[2,544,128]{2,1,0:T(8,128)S(1)}) custom-call(f32[512,256]{1,0:T(8,128)} %b.5, f32[512,256]{1,0:T(8,128)} %cr.5), custom_call_target="tpu_custom_call" | custom-call | tf_op jit(solution)/shard_map/own/pallas_call | solution.py:452
  13.5 4.1 %collective-permute-done.refs_0_ = f32[160,256]{1,0:T(8,128)S(1)} collective-permute-done((f32[160,256]{1,0:T(8,128)S(1)}, f32[160,256]{1,0:T(8,128)S(1)}, u32[]{:S(2)}, u32[]{:S(2)}) %collective-permute-start) | collective-permute-done | bytes 163872 | tf_op jit(solution)/shard_map/ppermute | solution.py:38
  17.6 0.8 %step0.1 = (f32[2,560,128]{2,1,0:T(8,128)S(1)}, f32[2,544,128]{2,1,0:T(8,128)S(1)}, f32[2,544,128]{2,1,0:T(8,128)S(1)}, f32[8,560,128]{2,1,0:T(8,128)S(1)}, f32[...) custom-call(f32[160,256]{1,0:T(8,128)S(1)} %collective-permute-done., ...), custom_call_target="tpu_custom_call", output_to_operand_aliasing={{0}: (1, {}), {1}: (2, {}), {2}: (3, {})} | custom-call | tf_op jit(solution)/shard_map/step0/pallas_call | solution.py:490
  18.4 1.0 %collective-permute-done.1.refs_1_ = f32[136,256]{1,0:T(8,128)S(1)} collective-permute-done((f32[136,256]{1,0:T(8,128)S(1)}, f32[136,256]{1,0:T(8,128)S(1)}, u32[]{:S(2)}, u32[]{:S(2)}) %collective-permute-start.1) | collective-permute-done | bytes 139296 | tf_op jit(solution)/shard_map/ppermute | solution.py:38
  19.4 0.6 %step1.1 = (f32[2,560,128]{2,1,0:T(8,128)S(1)}, f32[2,544,128]{2,1,0:T(8,128)S(1)}, f32[2,544,128]{2,1,0:T(8,128)S(1)}, f32[8,560,128]{2,1,0:T(8,128)S(1)}, f32[...) custom-call(f32[160,256]{1,0:T(8,128)S(1)} %collective-permute-done., ...), custom_call_target="tpu_custom_call", output_to_operand_aliasing={{0}: (2, {}), {1}: (3, {}), {2}: (4, {}), {3}: (5, {}), {4}... | custom-call | tf_op jit(solution)/shard_map/step1/pallas_call | solution.py:490
  20.0 0.0 collective-permute-done.2.refs_2_
  20.0 1.3 %step2.1 = (f32[2,560,128]{2,1,0:T(8,128)S(1)}, f32[2,544,128]{2,1,0:T(8,128)S(1)}, f32[2,544,128]{2,1,0:T(8,128)S(1)}, f32[8,560,128]{2,1,0:T(8,128)S(1)}, f32[...) custom-call(f32[160,256]{1,0:T(8,128)S(1)} %collective-permute-done., ...), custom_call_target="tpu_custom_call", output_to_operand_aliasing={{0}: (3, {}), {1}: (4, {}), {2}: (5, {}), {3}: (6, {}), {4}... | custom-call | tf_op jit(solution)/shard_map/step2/pallas_call | solution.py:490
  21.3 0.0 collective-permute-done.4.refs_4_
  21.3 4.1 %collective-permute-done.3.refs_3_ = f32[56,256]{1,0:T(8,128)S(1)} collective-permute-done((f32[56,256]{1,0:T(8,128)S(1)}, f32[56,256]{1,0:T(8,128)S(1)}, u32[]{:S(2)}, u32[]{:S(2)}) %collective-permute-start.3) | collective-permute-done | bytes 57376 | tf_op jit(solution)/shard_map/ppermute | solution.py:38
  25.4 0.6 %step3.1 = (f32[2,560,128]{2,1,0:T(8,128)S(1)}, f32[2,544,128]{2,1,0:T(8,128)S(1)}, f32[2,544,128]{2,1,0:T(8,128)S(1)}, f32[8,560,128]{2,1,0:T(8,128)S(1)}, f32[...) custom-call(f32[160,256]{1,0:T(8,128)S(1)} %collective-permute-done., ...), custom_call_target="tpu_custom_call", output_to_operand_aliasing={{0}: (5, {}), {1}: (6, {}), {2}: (7, {}), {3}: (8, {}), {4}... | custom-call | tf_op jit(solution)/shard_map/step3/pallas_call | solution.py:490
  26.0 12.4 %all_to_all.11 = f32[32,1,128]{2,1,0:T(1,128)S(1)} all-to-all(f32[32,1,128]{2,1,0:T(1,128)S(1)} %bitcast.7), channel_id=1, replica_groups=mesh['circ'=4,'radax'=8] {'circ','radax'}, dimensions={0} | all-to-all | bytes 32768 | tf_op jit(solution)/shard_map/all_to_all | solution.py:506
  38.4 1.3 %finish.1 = (f32[512,256]{1,0:T(8,128)}, f32[512,256]{1,0:T(8,128)}) custom-call(f32[32,128]{1,0:T(8,128)S(1)} %bitcast.6, f32[2,560,128]{2,1,0:T(8,128)S(1)} %get-tuple-element.87.trace, f32[2,560,128]{2,1,0:T(8,128)S(1)} %get-tuple-element.88.image, f32[2,512,128]{2,1,0:T(8,128)S(1)} %get-tuple-element.89.second), custom_call_target="tpu_custom_call" | custom-call | tf_op jit(solution)/shard_map/finish/pallas_call | solution.py:508
Async XLA Ops:
  1.6 18.4 %collective-permute-start.2 = (f32[216,256]{1,0:T(8,128)S(1)}, f32[216,256]{1,0:T(8,128)S(1)}, u32[]{:S(2)}, u32[]{:S(2)}) collective-permute-start(f32[216,256]{1,0:T(8,128)S(1)} %pack.2.refs_0_), channel_id=1, source_target_pairs={{16,0},{24,8},{0,16},{8,24},{17,1},{25,9},{1,17},{9,25},{18,2},{26... | collective-permute-start | bytes 663560 | tf_op jit(solution)/shard_map/ppermute | solution.py:38
  6.9 10.8 %collective-permute-start = (f32[160,256]{1,0:T(8,128)S(1)}, f32[160,256]{1,0:T(8,128)S(1)}, u32[]{:S(2)}, u32[]{:S(2)}) collective-permute-start(f32[160,256]{1,0:T(8,128)S(1)} %get-tuple-element.46), channel_id=1, source_target_pairs={{8,0},{16,8},{24,16},{0,24},{9,1},{17,9},{25,17},{1,25},{10,2},{18... | collective-permute-start | bytes 491528 | tf_op jit(solution)/shard_map/ppermute | solution.py:38
  8.3 11.1 %collective-permute-start.1 = (f32[136,256]{1,0:T(8,128)S(1)}, f32[136,256]{1,0:T(8,128)S(1)}, u32[]{:S(2)}, u32[]{:S(2)}) collective-permute-start(f32[136,256]{1,0:T(8,128)S(1)} %get-tuple-element.47), channel_id=1, source_target_pairs={{8,0},{16,8},{24,16},{0,24},{9,1},{17,9},{25,17},{1,25},{10,2},{18... | collective-permute-start | bytes 417800 | tf_op jit(solution)/shard_map/ppermute | solution.py:38
  8.4 17.0 %collective-permute-start.3 = (f32[56,256]{1,0:T(8,128)S(1)}, f32[56,256]{1,0:T(8,128)S(1)}, u32[]{:S(2)}, u32[]{:S(2)}) collective-permute-start(f32[56,256]{1,0:T(8,128)S(1)} %get-tuple-element.48), channel_id=1, source_target_pairs={{16,0},{24,8},{0,16},{8,24},{17,1},{25,9},{1,17},{9,25},{18,2},{26... | collective-permute-start | bytes 172040 | tf_op jit(solution)/shard_map/ppermute | solution.py:38
  10.4 10.9 %collective-permute-start.4 = (f32[24,256]{1,0:T(8,128)S(1)}, f32[24,256]{1,0:T(8,128)S(1)}, u32[]{:S(2)}, u32[]{:S(2)}) collective-permute-start(f32[24,256]{1,0:T(8,128)S(1)} %get-tuple-element.49), channel_id=1, source_target_pairs={{24,0},{0,8},{8,16},{16,24},{25,1},{1,9},{9,17},{17,25},{26,2},{2,... | collective-permute-start | bytes 73736 | tf_op jit(solution)/shard_map/ppermute | solution.py:38

commit v8 on v7

--- a/solution.py
+++ b/solution.py
@@ -19,7 +19,7 @@
 TAPS = range(-REACH, REACH + 2)
 CHUNK = 16
 WRITES = 4
-LATER = (1, 5), (1, 2)
+LATER = (1, 5), (3, 8)
 VMEM = pl.BlockSpec(memory_space=pltpu.VMEM)
 PARAMS = pltpu.CompilerParams(vmem_limit_bytes=40 << 20)
 

time: 39.9 us -> 39.9 us (level)
  no operation moved by 1% of the time
where the time goes in v8:
time: 39.9 us; the launch traced here: 39.7 us
  blocking collectives  12.4 us (31%)
  starting transfers between devices  9.22 us (23%)
  waiting for transfers between devices  9.18 us (23%)
  Pallas kernels  8.21 us (21%)
  between operations  0.69 us (2%)
    all_to_all x1, blocking collectives, local(): parts = lax.all_to_all(line, ('circ', 'radax'), 0, 0, tiled=True)  12.4 us
    ppermute x5, starting transfers between devices, shifted(): return lax.ppermute(block, 'circ', route)  9.22 us
    ppermute x5, waiting for transfers between devices, shifted(): return lax.ppermute(block, 'circ', route)  9.18 us
    pallas_call x4, Pallas kernels, local(): pl.pallas_call(functools.partial(step_kernel, rows, opening, closing, wor...  3.22 us
    pallas_call x2, Pallas kernels, pack(): pl.pallas_call(functools.partial(pack_kernel, rows, total_rows, laid), ou...  2.13 us
    pallas_call x1, Pallas kernels, local(): pl.pallas_call(functools.partial(own_kernel, rows), out_shape=[shapes['tr...  1.55 us
    pallas_call x1, Pallas kernels, local(): pl.pallas_call(functools.partial(finish_kernel, rows, groups), out_shape=...  1.31 us
  transfers between devices with their start and end apart: 5, of which 3 were waited for; matrix products, arithmetic and copies ran while one was open for 0% of the time, Pallas kernels for 13%

profile of v8, /device:TPU:0, one launch (start us, length us, event | category | flops | bytes accessed | tf_op | source)
XLA Modules:
  0.0 39.7 jit_solution(17974401704328463686)
XLA Ops:
  0.6 1.0 %pack.2.refs_0_ = f32[216,256]{1,0:T(8,128)S(1)} custom-call(f32[512,256]{1,0:T(8,128)} %b.5, f32[512,256]{1,0:T(8,128)} %cr.5, f32[512,256]{1,0:T(8,128)} %cs.3, s32[4,128]{1,0:T(4,128)} %bitcast.8, f32[4,128]{1,0:T(4,128)} %bitcast.10), custom_call_target="tpu_custom_call" | custom-call | tf_op jit(solution)/shard_map/pack/pallas_call | solution.py:419
  1.6 4.1 %collective-permute-start.2 = (f32[216,256]{1,0:T(8,128)S(1)}, f32[216,256]{1,0:T(8,128)S(1)}, u32[]{:S(2)}, u32[]{:S(2)}) collective-permute-start(f32[216,256]{1,0:T(8,128)S(1)} %pack.2.refs_0_), channel_id=1, source_target_pairs={{16,0},{24,8},{0,16},{8,24},{17,1},{25,9},{1,17},{9,25},{18,2},{26... | collective-permute-start | bytes 663560 | tf_op jit(solution)/shard_map/ppermute | solution.py:38
  5.7 1.1 %pack.3 = (f32[192,256]{1,0:T(8,128)S(1)}, f32[104,256]{1,0:T(8,128)S(1)}, f32[56,256]{1,0:T(8,128)S(1)}, f32[24,256]{1,0:T(8,128)S(1)}) custom-call(f32[512,256]{1,0:T(8,128)} %b.5, f32[512,256]{1,0:T(8,128)} %cr.5, f32[512,256]{1,0:T(8,128)} %cs.3, s32[4,128]{1,0:T(4,128)} %bitcast.9, f32[4,128]{1,0:T(4,128)} %bitcast.11, f32[216,256]{1,0:T(8,128)S(1)} %pack.2.refs_0_), custom_call_target="tpu_custom_call" | custom-call | tf_op jit(solution)/shard_map/pack/pallas_call | solution.py:419
  6.9 1.4 %collective-permute-start = (f32[192,256]{1,0:T(8,128)S(1)}, f32[192,256]{1,0:T(8,128)S(1)}, u32[]{:S(2)}, u32[]{:S(2)}) collective-permute-start(f32[192,256]{1,0:T(8,128)S(1)} %get-tuple-element.46), channel_id=1, source_target_pairs={{8,0},{16,8},{24,16},{0,24},{9,1},{17,9},{25,17},{1,25},{10,2},{18... | collective-permute-start | bytes 589832 | tf_op jit(solution)/shard_map/ppermute | solution.py:38
  8.3 0.1 collective-permute-start.1
  8.4 2.0 %collective-permute-start.3 = (f32[56,256]{1,0:T(8,128)S(1)}, f32[56,256]{1,0:T(8,128)S(1)}, u32[]{:S(2)}, u32[]{:S(2)}) collective-permute-start(f32[56,256]{1,0:T(8,128)S(1)} %get-tuple-element.48), channel_id=1, source_target_pairs={{16,0},{24,8},{0,16},{8,24},{17,1},{25,9},{1,17},{9,25},{18,2},{26... | collective-permute-start | bytes 172040 | tf_op jit(solution)/shard_map/ppermute | solution.py:38
  10.4 1.6 %collective-permute-start.4 = (f32[24,256]{1,0:T(8,128)S(1)}, f32[24,256]{1,0:T(8,128)S(1)}, u32[]{:S(2)}, u32[]{:S(2)}) collective-permute-start(f32[24,256]{1,0:T(8,128)S(1)} %get-tuple-element.49), channel_id=1, source_target_pairs={{24,0},{0,8},{8,16},{16,24},{25,1},{1,9},{9,17},{17,25},{26,2},{2,... | collective-permute-start | bytes 73736 | tf_op jit(solution)/shard_map/ppermute | solution.py:38
  12.0 1.6 %own.1 = (f32[2,560,128]{2,1,0:T(8,128)S(1)}, f32[2,544,128]{2,1,0:T(8,128)S(1)}, f32[2,544,128]{2,1,0:T(8,128)S(1)}) custom-call(f32[512,256]{1,0:T(8,128)} %b.5, f32[512,256]{1,0:T(8,128)} %cr.5), custom_call_target="tpu_custom_call" | custom-call | tf_op jit(solution)/shard_map/own/pallas_call | solution.py:452
  13.6 4.5 %collective-permute-done.refs_0_ = f32[192,256]{1,0:T(8,128)S(1)} collective-permute-done((f32[192,256]{1,0:T(8,128)S(1)}, f32[192,256]{1,0:T(8,128)S(1)}, u32[]{:S(2)}, u32[]{:S(2)}) %collective-permute-start) | collective-permute-done | bytes 196640 | tf_op jit(solution)/shard_map/ppermute | solution.py:38
  18.0 0.9 %step0.1 = (f32[2,560,128]{2,1,0:T(8,128)S(1)}, f32[2,544,128]{2,1,0:T(8,128)S(1)}, f32[2,544,128]{2,1,0:T(8,128)S(1)}, f32[8,560,128]{2,1,0:T(8,128)S(1)}, f32[...) custom-call(f32[192,256]{1,0:T(8,128)S(1)} %collective-permute-done., ...), custom_call_target="tpu_custom_call", output_to_operand_aliasing={{0}: (1, {}), {1}: (2, {}), {2}: (3, {})} | custom-call | tf_op jit(solution)/shard_map/step0/pallas_call | solution.py:490
  18.9 0.5 %collective-permute-done.1.refs_1_ = f32[104,256]{1,0:T(8,128)S(1)} collective-permute-done((f32[104,256]{1,0:T(8,128)S(1)}, f32[104,256]{1,0:T(8,128)S(1)}, u32[]{:S(2)}, u32[]{:S(2)}) %collective-permute-start.1) | collective-permute-done | bytes 106528 | tf_op jit(solution)/shard_map/ppermute | solution.py:38
  19.4 0.5 %step1.1 = (f32[2,560,128]{2,1,0:T(8,128)S(1)}, f32[2,544,128]{2,1,0:T(8,128)S(1)}, f32[2,544,128]{2,1,0:T(8,128)S(1)}, f32[8,560,128]{2,1,0:T(8,128)S(1)}, f32[...) custom-call(f32[192,256]{1,0:T(8,128)S(1)} %collective-permute-done., ...), custom_call_target="tpu_custom_call", output_to_operand_aliasing={{0}: (2, {}), {1}: (3, {}), {2}: (4, {}), {3}: (5, {}), {4}... | custom-call | tf_op jit(solution)/shard_map/step1/pallas_call | solution.py:490
  19.9 0.0 collective-permute-done.2.refs_2_
  19.9 1.3 %step2.1 = (f32[2,560,128]{2,1,0:T(8,128)S(1)}, f32[2,544,128]{2,1,0:T(8,128)S(1)}, f32[2,544,128]{2,1,0:T(8,128)S(1)}, f32[8,560,128]{2,1,0:T(8,128)S(1)}, f32[...) custom-call(f32[192,256]{1,0:T(8,128)S(1)} %collective-permute-done., ...), custom_call_target="tpu_custom_call", output_to_operand_aliasing={{0}: (3, {}), {1}: (4, {}), {2}: (5, {}), {3}: (6, {}), {4}... | custom-call | tf_op jit(solution)/shard_map/step2/pallas_call | solution.py:490
  21.2 0.0 collective-permute-done.4.refs_4_
  21.2 4.2 %collective-permute-done.3.refs_3_ = f32[56,256]{1,0:T(8,128)S(1)} collective-permute-done((f32[56,256]{1,0:T(8,128)S(1)}, f32[56,256]{1,0:T(8,128)S(1)}, u32[]{:S(2)}, u32[]{:S(2)}) %collective-permute-start.3) | collective-permute-done | bytes 57376 | tf_op jit(solution)/shard_map/ppermute | solution.py:38
  25.4 0.6 %step3.1 = (f32[2,560,128]{2,1,0:T(8,128)S(1)}, f32[2,544,128]{2,1,0:T(8,128)S(1)}, f32[2,544,128]{2,1,0:T(8,128)S(1)}, f32[8,560,128]{2,1,0:T(8,128)S(1)}, f32[...) custom-call(f32[192,256]{1,0:T(8,128)S(1)} %collective-permute-done., ...), custom_call_target="tpu_custom_call", output_to_operand_aliasing={{0}: (5, {}), {1}: (6, {}), {2}: (7, {}), {3}: (8, {}), {4}... | custom-call | tf_op jit(solution)/shard_map/step3/pallas_call | solution.py:490
  26.0 12.4 %all_to_all.11 = f32[32,1,128]{2,1,0:T(1,128)S(1)} all-to-all(f32[32,1,128]{2,1,0:T(1,128)S(1)} %bitcast.7), channel_id=1, replica_groups=mesh['circ'=4,'radax'=8] {'circ','radax'}, dimensions={0} | all-to-all | bytes 32768 | tf_op jit(solution)/shard_map/all_to_all | solution.py:506
  38.4 1.3 %finish.1 = (f32[512,256]{1,0:T(8,128)}, f32[512,256]{1,0:T(8,128)}) custom-call(f32[32,128]{1,0:T(8,128)S(1)} %bitcast.6, f32[2,560,128]{2,1,0:T(8,128)S(1)} %get-tuple-element.87.trace, f32[2,560,128]{2,1,0:T(8,128)S(1)} %get-tuple-element.88.image, f32[2,512,128]{2,1,0:T(8,128)S(1)} %get-tuple-element.89.second), custom_call_target="tpu_custom_call" | custom-call | tf_op jit(solution)/shard_map/finish/pallas_call | solution.py:508
Async XLA Ops:
  1.6 18.3 %collective-permute-start.2 = (f32[216,256]{1,0:T(8,128)S(1)}, f32[216,256]{1,0:T(8,128)S(1)}, u32[]{:S(2)}, u32[]{:S(2)}) collective-permute-start(f32[216,256]{1,0:T(8,128)S(1)} %pack.2.refs_0_), channel_id=1, source_target_pairs={{16,0},{24,8},{0,16},{8,24},{17,1},{25,9},{1,17},{9,25},{18,2},{26... | collective-permute-start | bytes 663560 | tf_op jit(solution)/shard_map/ppermute | solution.py:38
  6.9 11.1 %collective-permute-start = (f32[192,256]{1,0:T(8,128)S(1)}, f32[192,256]{1,0:T(8,128)S(1)}, u32[]{:S(2)}, u32[]{:S(2)}) collective-permute-start(f32[192,256]{1,0:T(8,128)S(1)} %get-tuple-element.46), channel_id=1, source_target_pairs={{8,0},{16,8},{24,16},{0,24},{9,1},{17,9},{25,17},{1,25},{10,2},{18... | collective-permute-start | bytes 589832 | tf_op jit(solution)/shard_map/ppermute | solution.py:38
  8.3 11.1 %collective-permute-start.1 = (f32[104,256]{1,0:T(8,128)S(1)}, f32[104,256]{1,0:T(8,128)S(1)}, u32[]{:S(2)}, u32[]{:S(2)}) collective-permute-start(f32[104,256]{1,0:T(8,128)S(1)} %get-tuple-element.47), channel_id=1, source_target_pairs={{8,0},{16,8},{24,16},{0,24},{9,1},{17,9},{25,17},{1,25},{10,2},{18... | collective-permute-start | bytes 319496 | tf_op jit(solution)/shard_map/ppermute | solution.py:38
  8.4 17.0 %collective-permute-start.3 = (f32[56,256]{1,0:T(8,128)S(1)}, f32[56,256]{1,0:T(8,128)S(1)}, u32[]{:S(2)}, u32[]{:S(2)}) collective-permute-start(f32[56,256]{1,0:T(8,128)S(1)} %get-tuple-element.48), channel_id=1, source_target_pairs={{16,0},{24,8},{0,16},{8,24},{17,1},{25,9},{1,17},{9,25},{18,2},{26... | collective-permute-start | bytes 172040 | tf_op jit(solution)/shard_map/ppermute | solution.py:38
  10.4 10.8 %collective-permute-start.4 = (f32[24,256]{1,0:T(8,128)S(1)}, f32[24,256]{1,0:T(8,128)S(1)}, u32[]{:S(2)}, u32[]{:S(2)}) collective-permute-start(f32[24,256]{1,0:T(8,128)S(1)} %get-tuple-element.49), channel_id=1, source_target_pairs={{24,0},{0,8},{8,16},{16,24},{25,1},{1,9},{9,17},{17,25},{26,2},{2,... | collective-permute-start | bytes 73736 | tf_op jit(solution)/shard_map/ppermute | solution.py:38
